TPU v7x, 32 devices: a whole 2x2x4 slice. The times are simulated.
32 devices in a mesh: req: 4 (over x, core), kv: 8 (over z, y).
Axes of the slice: x: 2, y: 2, z: 4, core: 2. Of those that a mesh axis runs over, the one named last changes fastest.
Arguments:
- x_steps: bfloat16 [4, 256, 1536], P(None, ('req', 'kv')), may hold values from -6 to 6
- lengths: int32 [32], replicated, may hold values from 16 to 8192
- perm: int32 [32], replicated, may hold values from 0 to 31, as said below
- parents: int32 [4, 256], replicated, may hold values from 0 to 7
- table: int32 [256, 9], P(('req', 'kv')), may hold values from 0 to 2303, as said below
- pool: bfloat16 [2304, 128, 256], P(('req', 'kv')), may hold values from -900 to 900
- norm_attn: float32 [1536], replicated, may hold values from 0.1 to 1.9
- w_query: bfloat16 [1536, 1536], replicated, may hold values from -0.15625 to 0.15625
- w_keyval: bfloat16 [1536, 256], replicated, may hold values from -0.15625 to 0.15625
- w_out: bfloat16 [1536, 1536], replicated, may hold values from -0.15625 to 0.15625
- norm_mlp: float32 [1536], replicated, may hold values from 0.1 to 1.9
- w_gate: bfloat16 [1536, 4608], P(None, 'kv'), may hold values from -0.15625 to 0.15625
- w_up: bfloat16 [1536, 4608], P(None, 'kv'), may hold values from -0.15625 to 0.15625
- w_down: bfloat16 [4608, 1536], P('kv'), may hold values from -0.09375 to 0.09375
Outputs:
- outputs: bfloat16 [4, 256, 1536], P(None, ('req', 'kv'))
Inputs may be any that keep to these rules, and one draw needn't show every extreme that they name: perm is a permutation with perm[s] % 8 == s % 8; among the 8 slots s with one s // 8 and one s % 8 // 8, every req index occurs as perm[s] // 8 exactly once. The entries of row b lie in [(b // 8) * 72, (b // 8 + 1) * 72); no page appears twice in the table.
All inputs are finite; a program needn't handle non-finite values.
Results may differ from a plain program's by a relative error of at most 0.02.
Values may be sent and summed in bfloat16 or wider, within the bound.
A program may use at most 192 MiB of HBM per device.

v0:
```python
import jax
import jax.numpy as jnp
from jax import lax
from jax.sharding import PartitionSpec as P

WINDOW = 1024
PAGE = 128
BEAMS = 8


EPSILON = 1e-06
NEGATIVE = -1e30


def merged_2(array, axis, combine):
    everything = jax.tree.map(lambda part: lax.all_gather(part, axis), array)
    first = jax.tree.map(lambda part: part[0], everything)

    def turn(k, so_far):
        return combine(so_far, jax.tree.map(lambda part: part[k], everything))

    return lax.fori_loop(1, lax.axis_size(axis), turn, first)


def member_of(beam_index, half_index, halves):
    return beam_index % 2 + 2 * half_index + 2 * halves * (beam_index // 2)


def rms_round(values, gain):
    wide = values.astype(jnp.float32)
    mean_square = jnp.mean(wide * wide, axis=-1, keepdims=True)
    return (wide * lax.rsqrt(mean_square + EPSILON) * gain).astype(jnp.bfloat16)


def page_partial(queries, pages, key_pos, length, step_index):
    head_dim = queries.shape[-1]
    keys = pages[:, :, :head_dim]
    values = pages[:, :, head_dim:]
    scores = jnp.einsum(
        "jrhd,rkd->jrhk", queries, keys, preferred_element_type=jnp.float32
    ) * head_dim ** (-0.5)
    allowed = (key_pos < length[:, None]) & (key_pos > length[:, None] + step_index - WINDOW)
    scores = jnp.where(allowed[None, :, None, :], scores, NEGATIVE)
    highest = jnp.max(scores, axis=-1)
    weights = jnp.exp(scores - highest[..., None]).astype(jnp.bfloat16)
    totals = jnp.sum(weights.astype(jnp.float32), axis=-1)
    weighted = jnp.einsum("jrhk,rkd->jrhd", weights, values, preferred_element_type=jnp.float32)
    return (highest, totals, weighted)


def fresh_partial(queries, entries, count):
    head_dim = queries.shape[-1]
    keys = entries[..., :count, :head_dim]
    values = entries[..., :count, head_dim:]
    scores = jnp.einsum(
        "...hd,...kd->...hk", queries, keys, preferred_element_type=jnp.float32
    ) * head_dim ** (-0.5)
    highest = jnp.max(scores, axis=-1)
    weights = jnp.exp(scores - highest[..., None]).astype(jnp.bfloat16)
    totals = jnp.sum(weights.astype(jnp.float32), axis=-1)
    weighted = jnp.einsum("...hk,...kd->...hd", weights, values, preferred_element_type=jnp.float32)
    return (highest, totals, weighted)


def join_parts(first, second):
    highest = jnp.maximum(first[0], second[0])
    scale_first = jnp.exp(first[0] - highest)
    scale_second = jnp.exp(second[0] - highest)
    totals = first[1] * scale_first + second[1] * scale_second
    weighted = first[2] * scale_first[..., None] + second[2] * scale_second[..., None]
    return (highest, totals, weighted)


def feed_forward(mlp_in, w_gate, w_up, w_down):
    gate = jnp.dot(mlp_in, w_gate, preferred_element_type=jnp.float32)
    upward = jnp.dot(mlp_in, w_up, preferred_element_type=jnp.float32)
    hidden = (jax.nn.gelu(gate, approximate=True) * upward).astype(jnp.bfloat16)
    return jnp.dot(hidden, w_down, preferred_element_type=jnp.float32)


def rank_within(labels, offsets):
    earlier = (labels[None, :] == labels[:, None]) & (offsets[None, :] < offsets[:, None])
    return jnp.sum(earlier.astype(jnp.int32), axis=1)


def pick_half(array, halves, half):
    shaped = array.reshape((BEAMS // 2, halves, 2) + array.shape[1:])
    picked = lax.dynamic_index_in_dim(shaped, half, 1, keepdims=False)
    return picked.reshape((BEAMS,) + array.shape[1:])


def place_block(block, filler, halves, half):
    whole = jnp.full((BEAMS // 2, halves, 2) + block.shape[1:], filler, block.dtype)
    placed = lax.dynamic_update_slice_in_dim(
        whole, block.reshape((BEAMS // 2, 1, 2) + block.shape[1:]), half, 1
    )
    return placed.reshape((BEAMS * halves,) + block.shape[1:])


def on_device(
    x_steps,
    lengths,
    perm,
    parents,
    table,
    pool,
    norm_attn,
    w_query,
    w_keyval,
    w_out,
    norm_mlp,
    w_gate,
    w_up,
    w_down,
):
    steps, rows, width = x_steps.shape
    head_dim = pool.shape[2] // 2
    heads = w_query.shape[1] // head_dim
    span = table.shape[1] * pool.shape[1]
    req_count = lax.axis_size("req")
    kv_count = lax.axis_size("kv")
    group = lax.axis_index("req")
    member = lax.axis_index("kv")
    halves = kv_count // BEAMS
    half = member // 2 % halves
    beam = member % 2 + 2 * (member // (2 * halves))
    per_group = halves * rows
    group_rows = kv_count * rows
    quota = rows // req_count
    offsets = jnp.arange(rows, dtype=jnp.int32)
    slot_ids = group * per_group + half * rows + offsets
    placed = lax.dynamic_slice_in_dim(perm.reshape(req_count, per_group), half * rows, rows, 1)
    serving = lax.dynamic_index_in_dim(placed, group, 0, keepdims=False)
    target = jnp.sum(
        jnp.where(placed == slot_ids[None, :], jnp.arange(req_count, dtype=jnp.int32)[:, None], 0),
        axis=0,
    )
    anchor = serving // per_group
    send_order = jnp.argsort(target * rows + offsets)
    outgoing = x_steps[:, send_order].reshape(steps, req_count, quota, width)
    arrived = lax.all_to_all(outgoing, "req", split_axis=1, concat_axis=1, tiled=True).reshape(
        steps, rows, width
    )
    inputs = arrived[:, anchor * quota + rank_within(anchor, offsets)]
    length = lengths[serving]
    first_page = jnp.maximum(length - WINDOW + 1, 0) // PAGE
    key_pos = first_page[:, None] * PAGE + jnp.arange(span, dtype=jnp.int32)[None, :]
    device = group * kv_count + member
    pages = pool[table - device * pool.shape[0]].reshape(rows, span, 2 * head_dim)
    family = lax.dynamic_slice_in_dim(parents, group * group_rows, group_rows, 1)
    row_ids = jnp.arange(group_rows, dtype=jnp.int32)
    row_member = row_ids // rows
    row_half = row_member // 2 % halves
    within = row_ids % rows
    ancestor = row_member % 2 + 2 * (row_member // (2 * halves))
    recent = jnp.zeros((group_rows, steps, 2 * head_dim), jnp.bfloat16)
    results = []
    for step_index in range(steps):
        parent_rows = member_of(family[step_index], row_half, halves) * rows + within
        ancestor = ancestor[parent_rows]
        recent = recent[parent_rows]
        current = inputs[step_index]
        normed = rms_round(current, norm_attn)
        query = jnp.dot(normed, w_query, preferred_element_type=jnp.float32).astype(jnp.bfloat16)
        fresh = jnp.dot(normed, w_keyval, preferred_element_type=jnp.float32).astype(jnp.bfloat16)
        query_all, fresh_all = (
            lax.all_gather(query, "kv", axis=0, tiled=True),
            lax.all_gather(fresh, "kv", axis=0, tiled=True),
        )
        recent = recent.at[:, step_index].set(fresh_all)
        query_block = pick_half(query_all.reshape(kv_count, rows, heads, head_dim), halves, half)
        held = pick_half(ancestor.reshape(kv_count, rows), halves, half) == beam
        page = page_partial(query_block, pages, key_pos, length, step_index)
        held_heads = held[..., None]
        highest = place_block(jnp.where(held_heads, page[0], NEGATIVE), NEGATIVE, halves, half)
        totals = place_block(jnp.where(held_heads, page[1], 0.0), 0.0, halves, half)
        weighted = place_block(jnp.where(held_heads[..., None], page[2], 0.0), 0.0, halves, half)
        merged = merged_2((highest, totals, weighted), "kv", join_parts)
        page_own = tuple(
            (
                lax.dynamic_index_in_dim(member_part, member, 0, keepdims=False)
                for member_part in merged
            )
        )
        own_entries = lax.dynamic_slice_in_dim(recent, member * rows, rows, 0)
        joined = join_parts(
            page_own,
            fresh_partial(query.reshape(rows, heads, head_dim), own_entries, step_index + 1),
        )
        attended = (
            (joined[2] / joined[1][..., None]).astype(jnp.bfloat16).reshape(rows, heads * head_dim)
        )
        residual = (
            current.astype(jnp.float32)
            + jnp.dot(attended, w_out, preferred_element_type=jnp.float32)
        ).astype(jnp.bfloat16)
        terms = feed_forward(
            lax.all_gather(rms_round(residual, norm_mlp), "kv", axis=0, tiled=True),
            w_gate,
            w_up,
            w_down,
        )
        summed = lax.psum_scatter(
            terms.astype(jnp.bfloat16), "kv", scatter_dimension=0, tiled=True
        ).astype(jnp.float32)
        results.append((residual.astype(jnp.float32) + summed).astype(jnp.bfloat16))
    finished = jnp.stack(results)
    back_order = jnp.argsort(anchor * rows + offsets)
    leaving = finished[:, back_order].reshape(steps, req_count, quota, width)
    returned = lax.all_to_all(leaving, "req", split_axis=1, concat_axis=1, tiled=True).reshape(
        steps, rows, width
    )
    return returned[:, target * quota + rank_within(target, offsets)]


def solution(mesh):
    in_specs = (
        P(None, ("req", "kv"), None),
        P(),
        P(),
        P(),
        P(("req", "kv"), None),
        P(("req", "kv"), None, None),
        P(),
        P(),
        P(),
        P(),
        P(),
        P(None, "kv"),
        P(None, "kv"),
        P("kv", None),
    )
    out_specs = P(None, ("req", "kv"), None)
    return jax.shard_map(
        on_device, mesh=mesh, in_specs=in_specs, out_specs=out_specs, check_vma=False
    )
```

profile of v0, /device:TPU:0, one launch (start us, length us, event | category | flops | bytes accessed | tf_op | source)
XLA Modules:
  0.0 1014.1 jit_solution(2502287649346980791)
XLA Ops:
  32.3 31.7 %all_gather.72 = bf16[64,1536]{1,0:T(8,128)(2,1)S(1)} all-gather(bf16[8,1536]{1,0:T(8,128)(2,1)S(1)} %convolution_convert_fusion.7), channel_id=1, replica_groups=mesh['req'=4,'kv'=8] {'kv'}, dimensions={0}, use_global_device_ids=true | all-gather | bytes 221184 | tf_op jit(solution)/shard_map/all_gather | solution.py:167
  72.7 31.4 %all_gather.78 = bf16[64,1536]{1,0:T(8,128)(2,1)S(1)} all-gather(bf16[8,1536]{1,0:T(8,128)(2,1)S(1)} %convolution_convert_fusion.6), channel_id=1, replica_groups=mesh['req'=4,'kv'=8] {'kv'}, dimensions={0}, use_global_device_ids=true | all-gather | bytes 221184 | tf_op jit(solution)/shard_map/all_gather | solution.py:167
  119.4 31.3 %all_gather.90 = bf16[64,1536]{1,0:T(8,128)(2,1)S(1)} all-gather(bf16[8,1536]{1,0:T(8,128)(2,1)S(1)} %convolution_convert_fusion.4), channel_id=1, replica_groups=mesh['req'=4,'kv'=8] {'kv'}, dimensions={0}, use_global_device_ids=true | all-gather | bytes 221184 | tf_op jit(solution)/shard_map/all_gather | solution.py:167
  156.9 30.8 %all_gather.76 = bf16[64,256]{1,0:T(8,128)(2,1)S(1)} all-gather(bf16[8,256]{1,0:T(8,128)(2,1)S(1)} %convolution_convert_fusion.11), channel_id=1, replica_groups=mesh['req'=4,'kv'=8] {'kv'}, dimensions={0}, use_global_device_ids=true | all-gather | bytes 36864 | tf_op jit(solution)/shard_map/all_gather | solution.py:168
  189.7 30.7 %all_gather.82 = bf16[64,256]{1,0:T(8,128)(2,1)S(1)} all-gather(bf16[8,256]{1,0:T(8,128)(2,1)S(1)} %convolution_convert_fusion.10), channel_id=1, replica_groups=mesh['req'=4,'kv'=8] {'kv'}, dimensions={0}, use_global_device_ids=true | all-gather | bytes 36864 | tf_op jit(solution)/shard_map/all_gather | solution.py:168
  222.3 30.4 %all_gather.88 = bf16[64,256]{1,0:T(8,128)(2,1)S(1)} all-gather(bf16[8,256]{1,0:T(8,128)(2,1)S(1)} %convolution_convert_fusion.9), channel_id=1, replica_groups=mesh['req'=4,'kv'=8] {'kv'}, dimensions={0}, use_global_device_ids=true | all-gather | bytes 36864 | tf_op jit(solution)/shard_map/all_gather | solution.py:168
  255.2 30.5 %all_gather.94 = bf16[64,256]{1,0:T(8,128)(2,1)S(1)} all-gather(bf16[8,256]{1,0:T(8,128)(2,1)S(1)} %convolution_convert_fusion.8), channel_id=1, replica_groups=mesh['req'=4,'kv'=8] {'kv'}, dimensions={0}, use_global_device_ids=true | all-gather | bytes 36864 | tf_op jit(solution)/shard_map/all_gather | solution.py:168
  299.2 31.5 %all_gather.84 = bf16[64,1536]{1,0:T(8,128)(2,1)S(1)} all-gather(bf16[8,1536]{1,0:T(8,128)(2,1)S(1)} %convolution_convert_fusion.5), channel_id=1, replica_groups=mesh['req'=4,'kv'=8] {'kv'}, dimensions={0}, use_global_device_ids=true | all-gather | bytes 221184 | tf_op jit(solution)/shard_map/all_gather | solution.py:167
  337.5 32.2 %all_gather.91 = f32[8,8,8,12]{3,2,1,0:T(8,128)S(1)} all-gather(f32[1,8,8,12]{3,2,1,0:T(8,128)S(1)} %copy.193), channel_id=1, replica_groups=mesh['req'=4,'kv'=8] {'kv'}, dimensions={0}, use_global_device_ids=true | all-gather | bytes 27648 | tf_op jit(solution)/shard_map/all_gather | solution.py:16
  369.8 30.7 %all_gather.92 = f32[8,8,8,12]{3,2,1,0:T(8,128)S(1)} all-gather(f32[1,8,8,12]{3,2,1,0:T(8,128)S(1)} %copy.194), channel_id=1, replica_groups=mesh['req'=4,'kv'=8] {'kv'}, dimensions={0}, use_global_device_ids=true | all-gather | bytes 27648 | tf_op jit(solution)/shard_map/all_gather | solution.py:16
  400.5 30.7 %all_gather.73 = f32[8,8,8,12]{3,2,1,0:T(8,128)S(1)} all-gather(f32[1,8,8,12]{3,2,1,0:T(8,128)S(1)} %copy.162), channel_id=1, replica_groups=mesh['req'=4,'kv'=8] {'kv'}, dimensions={0}, use_global_device_ids=true | all-gather | bytes 27648 | tf_op jit(solution)/shard_map/all_gather | solution.py:16
  431.3 30.8 %all_gather.74 = f32[8,8,8,12]{3,2,1,0:T(8,128)S(1)} all-gather(f32[1,8,8,12]{3,2,1,0:T(8,128)S(1)} %copy.163), channel_id=1, replica_groups=mesh['req'=4,'kv'=8] {'kv'}, dimensions={0}, use_global_device_ids=true | all-gather | bytes 27648 | tf_op jit(solution)/shard_map/all_gather | solution.py:16
  462.0 30.7 %all_gather.79 = f32[8,8,8,12]{3,2,1,0:T(8,128)S(1)} all-gather(f32[1,8,8,12]{3,2,1,0:T(8,128)S(1)} %copy.175), channel_id=1, replica_groups=mesh['req'=4,'kv'=8] {'kv'}, dimensions={0}, use_global_device_ids=true | all-gather | bytes 27648 | tf_op jit(solution)/shard_map/all_gather | solution.py:16
  492.8 30.7 %all_gather.80 = f32[8,8,8,12]{3,2,1,0:T(8,128)S(1)} all-gather(f32[1,8,8,12]{3,2,1,0:T(8,128)S(1)} %copy.176), channel_id=1, replica_groups=mesh['req'=4,'kv'=8] {'kv'}, dimensions={0}, use_global_device_ids=true | all-gather | bytes 27648 | tf_op jit(solution)/shard_map/all_gather | solution.py:16
  523.5 30.7 %all_gather.85 = f32[8,8,8,12]{3,2,1,0:T(8,128)S(1)} all-gather(f32[1,8,8,12]{3,2,1,0:T(8,128)S(1)} %copy.184), channel_id=1, replica_groups=mesh['req'=4,'kv'=8] {'kv'}, dimensions={0}, use_global_device_ids=true | all-gather | bytes 27648 | tf_op jit(solution)/shard_map/all_gather | solution.py:16
  554.2 30.9 %all_gather.86 = f32[8,8,8,12]{3,2,1,0:T(8,128)S(1)} all-gather(f32[1,8,8,12]{3,2,1,0:T(8,128)S(1)} %copy.185), channel_id=1, replica_groups=mesh['req'=4,'kv'=8] {'kv'}, dimensions={0}, use_global_device_ids=true | all-gather | bytes 27648 | tf_op jit(solution)/shard_map/all_gather | solution.py:16
  615.4 20.5 %while.81 = (s32[]{:T(128)}, f32[8,8,12]{2,1,0:T(8,128)S(1)}, f32[8,8,12]{2,1,0:T(8,128)}, f32[8,8,12,128]{3,2,1,0:T(8,128)S(1)}, f32[8,8,8,12]{3,2,1,0:T(8,128)...) while((s32[]{:T(128)}, f32[8,8,12]{2,1,0:T(8,128)S(1)}, ...), condition=%wide.region_14.15_spmd, body=%wide.region_13.14_spmd.sunk | while | flops 299525 | bytes 1341591 | solution.py:22
  670.9 26.5 %while.82 = (s32[]{:T(128)}, f32[8,8,12]{2,1,0:T(8,128)}, f32[8,8,12]{2,1,0:T(8,128)}, f32[8,8,12,128]{3,2,1,0:T(8,128)}, f32[8,8,8,12]{3,2,1,0:T(8,128)}, /*ind...) while((s32[]{:T(128)}, f32[8,8,12]{2,1,0:T(8,128)}, ...), condition=%wide.region_23.24_spmd, body=%wide.region_22.23_spmd.sunk | while | flops 299525 | bytes 1472663 | solution.py:22
  703.4 30.7 %all_gather.95 = bf16[64,1536]{1,0:T(8,128)(2,1)S(1)} all-gather(bf16[8,1536]{1,0:T(8,128)(2,1)S(1)} %get-tuple-element.1015), channel_id=1, replica_groups=mesh['req'=4,'kv'=8] {'kv'}, dimensions={0}, use_global_device_ids=true | all-gather | bytes 221184 | tf_op jit(solution)/shard_map/all_gather | solution.py:198
  739.5 31.0 %all_gather.89 = bf16[64,1536]{1,0:T(8,128)(2,1)S(1)} all-gather(bf16[8,1536]{1,0:T(8,128)(2,1)} %get-tuple-element.1014), channel_id=1, replica_groups=mesh['req'=4,'kv'=8] {'kv'}, dimensions={0}, use_global_device_ids=true | all-gather | bytes 221184 | tf_op jit(solution)/shard_map/all_gather | solution.py:198
  771.8 30.9 %all_gather.83 = bf16[64,1536]{1,0:T(8,128)(2,1)S(1)} all-gather(bf16[8,1536]{1,0:T(8,128)(2,1)} %get-tuple-element.1013), channel_id=1, replica_groups=mesh['req'=4,'kv'=8] {'kv'}, dimensions={0}, use_global_device_ids=true | all-gather | bytes 221184 | tf_op jit(solution)/shard_map/all_gather | solution.py:198
  808.2 32.9 %all_gather.77 = bf16[64,1536]{1,0:T(8,128)(2,1)} all-gather(bf16[8,1536]{1,0:T(8,128)(2,1)} %get-tuple-element.1012), channel_id=1, replica_groups=mesh['req'=4,'kv'=8] {'kv'}, dimensions={0}, use_global_device_ids=true | all-gather | bytes 221184 | tf_op jit(solution)/shard_map/all_gather | solution.py:198
  870.2 62.5 %reduce-scatter.7.cloned.1.call-done = bf16[8,1536]{1,0:T(8,128)(2,1)} async-done(((bf16[64,1536]{1,0:T(8,128)(2,1)}), bf16[8,1536]{1,0:T(8,128)(2,1)}) %reduce-scatter.7.cloned.1.call-update) | async-done | bytes 24592 | tf_op jit(solution)/shard_map/reduce_scatter | solution.py:203
  933.5 62.6 %reduce-scatter.5.cloned.1.call-done = bf16[8,1536]{1,0:T(8,128)(2,1)} async-done(((bf16[64,1536]{1,0:T(8,128)(2,1)}), bf16[8,1536]{1,0:T(8,128)(2,1)}) %reduce-scatter.5.cloned.1.call-update) | async-done | bytes 24592 | tf_op jit(solution)/shard_map/reduce_scatter | solution.py:203
  (364 shorter events, 284.4 us)
Async XLA Ops:
  6.5 729.6 %copy-start = (bf16[576,1536]{1,0:T(8,128)(2,1)S(1)}, bf16[576,1536]{1,0:T(8,128)(2,1)}, u32[]{:S(2)}) copy-start(bf16[576,1536]{1,0:T(8,128)(2,1)} %param.43) | copy-start | bytes 5308420
  10.9 17.2 %all-to-all-start = ((bf16[4,4,2,1536]{3,2,0,1:T(2,128)(2,1)}), bf16[4,4,2,1536]{3,2,0,1:T(2,128)(2,1)S(1)}, u32[]{:S(2)}, u32[]{:S(2)}) async-start(bf16[4,4,2,1536]{3,2,0,1:T(2,128)(2,1)} %copy.157), calls=%async_computation | async-start | bytes 196608 | tf_op jit(solution)/shard_map/all_to_all | solution.py:141
  15.1 580.6 %all-gather.9.cloned.1.call-start = ((), (), s32[]{:S(2)}) async-start(), calls=%async_computation.10 | async-start | bytes 4718592 | tf_op jit(solution)/shard_map/all_gather | solution.py:16
  28.8 638.2 %copy-start.9 = (bf16[8,4,1536]{2,0,1:T(8,128)(2,1)}, bf16[8,4,1536]{2,0,1:T(8,128)(2,1)S(1)}, u32[]{:S(2)}) copy-start(bf16[8,4,1536]{2,0,1:T(8,128)(2,1)S(1)} %copy.289) | copy-start | bytes 294916
  69.3 544.9 %all-gather.11.cloned.1.call-start = ((), (), s32[]{:S(2)}) async-start(), calls=%async_computation.11 | async-start | bytes 4718592 | tf_op jit(solution)/shard_map/all_gather | solution.py:16
  69.5 40.0 %slice-start.2 = ((s8[4718592]{0:T(1024)(128)(4,1)}), s8[4194304]{0:T(1024)(128)(4,1)S(1)}, s32[]{:S(2)}) async-start(s8[4718592]{0:T(1024)(128)(4,1)} %bitcast.523), calls=%async_computation.16 | async-start | bytes 8388608
  111.4 526.5 %all-gather.15.cloned.1.call-start = ((), (), s32[]{:S(2)}) async-start(), calls=%async_computation.13 | async-start | bytes 4718592 | tf_op jit(solution)/shard_map/all_gather | solution.py:16
  221.3 364.4 %copy-start.25 = (bf16[64,4,256]{2,1,0:T(4,128)(2,1)}, bf16[64,4,256]{2,1,0:T(4,128)(2,1)S(1)}, u32[]{:S(2)}) copy-start(bf16[64,4,256]{2,1,0:T(4,128)(2,1)S(1)} %scatter.15) | copy-start | bytes 393220
  253.6 334.4 %copy-start.24 = (bf16[64,4,256]{2,1,0:T(4,128)(2,1)}, bf16[64,4,256]{2,1,0:T(4,128)(2,1)S(1)}, u32[]{:S(2)}) copy-start(bf16[64,4,256]{2,1,0:T(4,128)(2,1)S(1)} %scatter.16) | copy-start | bytes 393220
  292.7 376.3 %all-gather.13.cloned.1.call-start = ((), (), s32[]{:S(2)}) async-start(), calls=%async_computation.12 | async-start | bytes 4718592 | tf_op jit(solution)/shard_map/all_gather | solution.py:16
  337.5 257.5 %copy-start.32 = (bf16[64,4,256]{2,1,0:T(4,128)(2,1)}, bf16[64,4,256]{2,1,0:T(4,128)(2,1)S(1)}, u32[]{:S(2)}) copy-start(bf16[64,4,256]{2,1,0:T(4,128)(2,1)S(1)} %scatter.19) | copy-start | bytes 393220
  369.8 218.5 %copy-start.17 = (f32[8,8,8,12]{3,2,1,0:T(8,128)}, f32[8,8,8,12]{3,2,1,0:T(8,128)S(1)}, u32[]{:S(2)}) copy-start(f32[8,8,8,12]{3,2,1,0:T(8,128)S(1)} %all_gather.91) | copy-start | bytes 73732
  400.5 187.8 %copy-start.18 = (f32[8,8,8,12]{3,2,1,0:T(8,128)}, f32[8,8,8,12]{3,2,1,0:T(8,128)S(1)}, u32[]{:S(2)}) copy-start(f32[8,8,8,12]{3,2,1,0:T(8,128)S(1)} %all_gather.92) | copy-start | bytes 73732
  431.2 158.3 %copy-start.21 = (f32[8,8,8,12]{3,2,1,0:T(8,128)}, f32[8,8,8,12]{3,2,1,0:T(8,128)S(1)}, u32[]{:S(2)}) copy-start(f32[8,8,8,12]{3,2,1,0:T(8,128)S(1)} %all_gather.73) | copy-start | bytes 73732
  462.0 127.6 %copy-start.22 = (f32[8,8,8,12]{3,2,1,0:T(8,128)}, f32[8,8,8,12]{3,2,1,0:T(8,128)S(1)}, u32[]{:S(2)}) copy-start(f32[8,8,8,12]{3,2,1,0:T(8,128)S(1)} %all_gather.74) | copy-start | bytes 73732
  492.8 95.6 %copy-start.19 = (f32[8,8,8,12]{3,2,1,0:T(8,128)}, f32[8,8,8,12]{3,2,1,0:T(8,128)S(1)}, u32[]{:S(2)}) copy-start(f32[8,8,8,12]{3,2,1,0:T(8,128)S(1)} %all_gather.79) | copy-start | bytes 73732
  523.5 65.5 %copy-start.20 = (f32[8,8,8,12]{3,2,1,0:T(8,128)}, f32[8,8,8,12]{3,2,1,0:T(8,128)S(1)}, u32[]{:S(2)}) copy-start(f32[8,8,8,12]{3,2,1,0:T(8,128)S(1)} %all_gather.80) | copy-start | bytes 73732
  554.2 40.8 %copy-start.15 = (f32[8,8,8,12]{3,2,1,0:T(8,128)}, f32[8,8,8,12]{3,2,1,0:T(8,128)S(1)}, u32[]{:S(2)}) copy-start(f32[8,8,8,12]{3,2,1,0:T(8,128)S(1)} %all_gather.85) | copy-start | bytes 73732
  595.1 255.0 %reduce-scatter.11.cloned.1.call-start = ((), (), s32[]{:S(2)}) async-start(), calls=%async_computation.9 | async-start | bytes 221184 | tf_op jit(solution)/shard_map/reduce_scatter | solution.py:203
  739.4 129.9 %reduce-scatter.9.cloned.1.call-start = ((), (), s32[]{:S(2)}) async-start(), calls=%async_computation.8 | async-start | bytes 221184 | tf_op jit(solution)/shard_map/reduce_scatter | solution.py:203
  808.1 124.6 %reduce-scatter.7.cloned.1.call-start = ((), (), s32[]{:S(2)}) async-start(), calls=%async_computation.7 | async-start | bytes 221184 | tf_op jit(solution)/shard_map/reduce_scatter | solution.py:203
  844.3 157.4 %copy-start.51 = (s32[8]{0:T(128)S(1)}, s32[8]{0:T(128)}, u32[]{:S(2)}) copy-start(s32[8]{0:T(128)} %fusion.206) | copy-start | bytes 100
  844.3 151.7 %reduce-scatter.5.cloned.1.call-start = ((), (), s32[]{:S(2)}) async-start(), calls=%async_computation.6 | async-start | bytes 221184 | tf_op jit(solution)/shard_map/reduce_scatter | solution.py:203
  998.4 7.6 all-to-all-start.1
  (42 other events, 398.8 us)
Sparse Core Ops, SparseCore 0:
  69.4 78.8 all-gather.8
  150.5 72.2 all-gather.10
  292.8 79.9 all-gather.14
  595.2 73.3 all-gather.12
  739.6 60.9 reduce-scatter.10
  808.2 61.0 reduce-scatter.8
  872.6 60.0 reduce-scatter.6
  935.9 60.1 reduce-scatter.4
where the time goes:
time: 1020 us; the launch traced here: 1010 us
  blocking collectives  622 us (61%)
  waiting for transfers between devices  148 us (15%)
  other arithmetic  102 us (10%)
  matrix products  72.1 us (7%)
  local copies, waits for them, and re-layouts  47.4 us (5%)
  between operations  14.6 us (1%)
    all_gather x8, blocking collectives, merged_2(): everything = jax.tree.map(lambda part: lax.all_gather(part, axis), array)  248 us
    reduce_scatter x4, waiting for transfers between devices, on_device(): lax.psum_scatter(terms.astype(jnp.bfloat16), 'kv', scatter_dimension=0, t...  144 us
    all_gather x4, blocking collectives, on_device(): lax.all_gather(query, 'kv', axis=0, tiled=True)  126 us
    all_gather x4, blocking collectives, on_device(): lax.all_gather(rms_round(residual, norm_mlp), 'kv', axis=0, tiled=True)  125 us
    all_gather x4, blocking collectives, on_device(): lax.all_gather(fresh, 'kv', axis=0, tiled=True)  123 us
    add x28, other arithmetic, join_parts(): first[2] * scale_first[..., None] + second[2] * scale_second[..., None]  46.9 us
    add x32, other arithmetic, join_parts(): totals = first[1] * scale_first + second[1] * scale_second  34.6 us
  transfers between devices with their start and end apart: 10, of which 4 were waited for; matrix products, arithmetic and copies ran while one was open for 15% of the time, Pallas kernels for 0%

commit v1 on v0

v1 whole, which is shorter than its diff:
```python
import functools

import jax
import jax.numpy as jnp
from jax import lax
from jax.experimental import pallas as pl
from jax.experimental.pallas import tpu as pltpu
from jax.sharding import PartitionSpec as P

WINDOW = 1024
PAGE = 128
BEAMS = 8


EPSILON = 1e-06
NEGATIVE = -1e30


def rms_round(values, gain):
    wide = values.astype(jnp.float32)
    mean_square = jnp.mean(wide * wide, axis=-1, keepdims=True)
    return (wide * lax.rsqrt(mean_square + EPSILON) * gain).astype(jnp.bfloat16)


def feed_forward(mlp_in, w_gate, w_up, w_down):
    gate = jnp.dot(mlp_in, w_gate, preferred_element_type=jnp.float32)
    upward = jnp.dot(mlp_in, w_up, preferred_element_type=jnp.float32)
    hidden = (jax.nn.gelu(gate, approximate=True) * upward).astype(jnp.bfloat16)
    return jnp.dot(hidden, w_down, preferred_element_type=jnp.float32)


def rank_within(labels, offsets):
    earlier = (labels[None, :] == labels[:, None]) & (offsets[None, :] < offsets[:, None])
    return jnp.sum(earlier.astype(jnp.int32), axis=1)


def pick_half(array, halves, half):
    if halves == 1:
        return array
    shaped = array.reshape((BEAMS // 2, halves, 2) + array.shape[1:])
    picked = lax.dynamic_index_in_dim(shaped, half, 1, keepdims=False)
    return picked.reshape((BEAMS,) + array.shape[1:])


def place_block(block, halves, half):
    if halves == 1:
        return block
    whole = jnp.zeros((BEAMS // 2, halves, 2) + block.shape[1:], block.dtype)
    placed = lax.dynamic_update_slice_in_dim(
        whole, block.reshape((BEAMS // 2, 1, 2) + block.shape[1:]), half, 1
    )
    return placed.reshape((BEAMS * halves,) + block.shape[1:])


def exchange(array, axis):
    return lax.all_to_all(array, axis, split_axis=0, concat_axis=0, tiled=True)


def gathered(block, axis):
    count = lax.axis_size(axis)
    return exchange(jnp.broadcast_to(block[None], (count,) + block.shape), axis)


def reordered(selector, array):
    return jnp.einsum(
        "pi,tiw->tpw", selector.astype(jnp.bfloat16), array, preferred_element_type=jnp.float32
    ).astype(jnp.bfloat16)


def attention_kernel(page_count, entries, table_ref, length_ref, *refs):
    pages = refs[:page_count]
    q_ref, new_ref, mask_ref, out_ref = refs[page_count:]
    row = pl.program_id(0)
    length = length_ref[row]
    head_dim = q_ref.shape[-1]
    span = page_count * PAGE
    queries = q_ref[0]
    marks = mask_ref[0].astype(jnp.float32)
    bias = marks[:, :entries]
    held = marks[:, entries : entries + 1]
    step = marks[:, entries + 1 : entries + 2].astype(jnp.int32)
    keys = jnp.concatenate([page[0, :, :head_dim] for page in pages], axis=0)
    values = jnp.concatenate([page[0, :, head_dim:] for page in pages], axis=0)
    first = jnp.maximum(length - WINDOW + 1, 0) // PAGE * PAGE
    shifted = lax.broadcasted_iota(jnp.int32, (1, span), 1) + (first - length + WINDOW)
    contract = (((1,), (1,)), ((), ()))
    scale = head_dim ** (-0.5)
    scores = lax.dot_general(queries, keys, contract, preferred_element_type=jnp.float32) * scale
    scores = jnp.where((shifted < WINDOW) & (shifted > step), scores, NEGATIVE)
    fresh = (
        lax.dot_general(
            queries, new_ref[0, :, :head_dim], contract, preferred_element_type=jnp.float32
        )
        * scale
    )
    fresh = jnp.where(bias > 0.5, fresh, NEGATIVE)
    highest = jnp.maximum(
        jnp.max(scores, axis=-1, keepdims=True), jnp.max(fresh, axis=-1, keepdims=True)
    )
    weights = jnp.exp(scores - highest).astype(jnp.bfloat16)
    fresh_weights = jnp.exp(fresh - highest).astype(jnp.bfloat16)
    totals = jnp.sum(weights.astype(jnp.float32), axis=-1, keepdims=True) + jnp.sum(
        fresh_weights.astype(jnp.float32), axis=-1, keepdims=True
    )
    weighted = jnp.dot(weights, values, preferred_element_type=jnp.float32) + jnp.dot(
        fresh_weights, new_ref[0, :, head_dim:], preferred_element_type=jnp.float32
    )
    out_ref[0] = jnp.where(held > 0.5, weighted / totals, 0.0).astype(jnp.bfloat16)


def attend(local_table, length, pool, queries, entries, marks):
    rows, count, head_dim = queries.shape
    page_count = local_table.shape[1]

    def page_spec(index):
        return pl.BlockSpec(
            (1, PAGE, 2 * head_dim),
            lambda row, table_ref, length_ref: (table_ref[row * page_count + index], 0, 0),
        )

    def row_spec(shape):
        return pl.BlockSpec((1,) + shape[1:], lambda row, table_ref, length_ref: (row, 0, 0))

    return pl.pallas_call(
        functools.partial(attention_kernel, page_count, entries.shape[1]),
        out_shape=jax.ShapeDtypeStruct((rows, count, head_dim), jnp.bfloat16),
        grid_spec=pltpu.PrefetchScalarGridSpec(
            num_scalar_prefetch=2,
            grid=(rows,),
            in_specs=[page_spec(index) for index in range(page_count)]
            + [row_spec(queries.shape), row_spec(entries.shape), row_spec(marks.shape)],
            out_specs=row_spec(queries.shape),
        ),
        compiler_params=pltpu.CompilerParams(vmem_limit_bytes=40 * 2**20),
    )(local_table.reshape(-1), length, *([pool] * page_count), queries, entries, marks)


def on_device(
    x_steps,
    lengths,
    perm,
    parents,
    table,
    pool,
    norm_attn,
    w_query,
    w_keyval,
    w_out,
    norm_mlp,
    w_gate,
    w_up,
    w_down,
):
    steps, rows, width = x_steps.shape
    head_dim = pool.shape[2] // 2
    heads = w_query.shape[1] // head_dim
    req_count = lax.axis_size("req")
    kv_count = lax.axis_size("kv")
    group = lax.axis_index("req")
    member = lax.axis_index("kv")
    halves = kv_count // BEAMS
    half = member // 2 % halves
    beam = member % 2 + 2 * (member // (2 * halves))
    per_group = halves * rows
    group_rows = kv_count * rows
    quota = rows // req_count
    offsets = jnp.arange(rows, dtype=jnp.int32)
    slot_ids = group * per_group + half * rows + offsets
    placed = lax.dynamic_slice_in_dim(perm.reshape(req_count, per_group), half * rows, rows, 1)
    serving = lax.dynamic_index_in_dim(placed, group, 0, keepdims=False)
    target = jnp.sum(
        jnp.where(placed == slot_ids[None, :], jnp.arange(req_count, dtype=jnp.int32)[:, None], 0),
        axis=0,
    )
    anchor = serving // per_group
    to_target = target * quota + rank_within(target, offsets)
    to_anchor = anchor * quota + rank_within(anchor, offsets)
    by_target = to_target[:, None] == offsets[None, :]
    by_anchor = to_anchor[:, None] == offsets[None, :]

    def swap(array):
        shaped = array.reshape(steps, req_count, quota, width)
        return lax.all_to_all(shaped, "req", split_axis=1, concat_axis=1, tiled=True).reshape(
            steps, rows, width
        )

    inputs = reordered(by_anchor, swap(reordered(by_target.T, x_steps)))
    current = inputs.reshape(steps * rows, width)
    length = lengths[serving]
    device = group * kv_count + member

    family = lax.dynamic_slice_in_dim(parents, group * group_rows, group_rows, 1)
    family = family.reshape(steps, kv_count, rows).transpose(1, 0, 2)
    family = pick_half(family, halves, half)
    beams = jnp.arange(BEAMS, dtype=jnp.int32)
    own = jnp.broadcast_to(beams[:, None], (BEAMS, rows))
    origins = [own]
    tables = []
    for step_index in range(steps):
        chosen = family[:, step_index][:, None, :] == beams[None, :, None]
        origins = [jnp.sum(jnp.where(chosen, origin[None], 0), axis=1) for origin in origins]
        origins.append(own)
        tables.append(
            jnp.stack(origins + [jnp.full_like(own, -1)] * (steps - 1 - step_index))
        )
    lineage = jnp.stack(tables)
    held = (lineage[:, 0] == beam).transpose(2, 1, 0)
    linked = lineage[:, 1:, :, :, None] == beams
    linked = linked.transpose(3, 2, 0, 4, 1).reshape(rows, BEAMS * steps, BEAMS * steps)
    step_marks = jnp.broadcast_to(
        jnp.arange(steps, dtype=jnp.int32), (rows, BEAMS, steps)
    )
    marks = jnp.concatenate(
        [
            linked.astype(jnp.bfloat16),
            held.reshape(rows, BEAMS * steps, 1).astype(jnp.bfloat16),
            step_marks.reshape(rows, BEAMS * steps, 1).astype(jnp.bfloat16),
        ],
        axis=2,
    )
    mark_count = marks.shape[2]
    marks = jnp.broadcast_to(
        marks[:, :, None, :], (rows, BEAMS * steps, heads, mark_count)
    ).reshape(rows, BEAMS * steps * heads, mark_count)

    normed = rms_round(current, norm_attn)
    query = jnp.dot(normed, w_query, preferred_element_type=jnp.float32).astype(jnp.bfloat16)
    fresh = jnp.dot(normed, w_keyval, preferred_element_type=jnp.float32).astype(jnp.bfloat16)
    sent = jnp.concatenate([query, fresh], axis=1)
    shared = pick_half(gathered(sent, "kv"), halves, half)
    shared = shared.reshape(BEAMS, steps, rows, -1).transpose(2, 0, 1, 3)
    queries = shared[..., : heads * head_dim].reshape(rows, BEAMS * steps * heads, head_dim)
    entries = shared[..., heads * head_dim :].reshape(rows, BEAMS * steps, 2 * head_dim)
    answers = attend(
        table - device * pool.shape[0], length, pool, queries, entries, marks
    )
    answers = answers.reshape(rows, BEAMS, steps, heads * head_dim).transpose(1, 2, 0, 3)
    returned = exchange(
        place_block(answers.reshape(BEAMS, steps * rows, heads * head_dim), halves, half), "kv"
    )
    attended = jnp.sum(returned.astype(jnp.float32), axis=0).astype(jnp.bfloat16)
    residual = (
        current.astype(jnp.float32) + jnp.dot(attended, w_out, preferred_element_type=jnp.float32)
    ).astype(jnp.bfloat16)
    everyone = gathered(rms_round(residual, norm_mlp), "kv").reshape(-1, width)
    terms = feed_forward(everyone, w_gate, w_up, w_down).astype(jnp.bfloat16)
    terms = exchange(terms.reshape(kv_count, steps * rows, width), "kv")
    summed = jnp.sum(terms.astype(jnp.float32), axis=0)
    finished = (residual.astype(jnp.float32) + summed).astype(jnp.bfloat16)
    finished = finished.reshape(steps, rows, width)
    return reordered(by_target, swap(reordered(by_anchor.T, finished)))


def solution(mesh):
    in_specs = (
        P(None, ("req", "kv"), None),
        P(),
        P(),
        P(),
        P(("req", "kv"), None),
        P(("req", "kv"), None, None),
        P(),
        P(),
        P(),
        P(),
        P(),
        P(None, "kv"),
        P(None, "kv"),
        P("kv", None),
    )
    out_specs = P(None, ("req", "kv"), None)
    return jax.shard_map(
        on_device, mesh=mesh, in_specs=in_specs, out_specs=out_specs, check_vma=False
    )
```

time: 1020 us -> 156 us (0.15)
  blocking collectives: 622 us -> 76.5 us
  waiting for transfers between devices: 148 us -> 23.1 us
  other arithmetic: 102 us -> 1.95 us
  matrix products: 72.1 us -> 14.8 us
  local copies, waits for them, and re-layouts: 47.4 us -> 15.5 us
  between operations: 14.6 us -> 0.47 us
  Pallas kernels: 0 us -> 11.9 us
    all_gather x20 -> x0, blocking collectives: 622 us -> none  [the longest x8 248 us: merged_2(): everything = jax.tree.map(lambda part: lax.all_gather(part, axis), array)]
    reduce_scatter x4 -> x0, waiting for transfers between devices: 144 us -> none  [on_device(): lax.psum_scatter(terms.astype(jnp.bfloat16), 'kv', scatter_dimension=0, t...]
    add x63 -> x2, other arithmetic: 81.5 us -> 0.02 us  [the longest x1 0.02 us: on_device(): to_anchor = anchor * quota + rank_within(anchor, offsets)]
    all_to_all x0 -> x4, blocking collectives: none -> 76.5 us  [the longest x3 69.9 us: exchange(): return lax.all_to_all(array, axis, split_axis=0, concat_axis=0, tiled=True)]
    dot_general x15 -> x4, matrix products: 26 us -> 2.49 us  [reordered(): jnp.einsum('pi,tiw->tpw', selector.astype(jnp.bfloat16), array, preferred...]
    gather x15 -> x0, local copies, waits for them, and re-layouts: 19.4 us -> none  [the longest x1 7.85 us: on_device(): pool[table - device * pool.shape[0]].reshape(rows, span, 2 * head_dim)]
    all_to_all x2, waiting for transfers between devices: 4.24 us -> 23.1 us  [the longest x1 21 us: exchange(): return lax.all_to_all(array, axis, split_axis=0, concat_axis=0, tiled=True)]
    pallas_call x0 -> x1, Pallas kernels: none -> 11.9 us  [attend(): pl.pallas_call(functools.partial(attention_kernel, page_count, entries.sh...]
  transfers between devices with their start and end apart: 10 -> 2, of which waited for: 4 -> 2; matrix products, arithmetic and copies ran while one was open for 15% -> 2% of each run, Pallas kernels for 0% -> 0%
where the time goes in v1:
time: 156 us; the launch traced here: 155 us
  blocking collectives  76.5 us (49%)
  waiting for transfers between devices  23.1 us (15%)
  local copies, waits for them, and re-layouts  15.5 us (10%)
  matrix products  14.8 us (9%)
  Pallas kernels  11.9 us (8%)
  starting transfers between devices  10.6 us (7%)
  other arithmetic  1.95 us (1%)
    all_to_all x3, blocking collectives, exchange(): return lax.all_to_all(array, axis, split_axis=0, concat_axis=0, tiled=True)  69.9 us
    all_to_all x1, waiting for transfers between devices, exchange(): return lax.all_to_all(array, axis, split_axis=0, concat_axis=0, tiled=True)  21 us
    pallas_call x1, Pallas kernels, attend(): pl.pallas_call(functools.partial(attention_kernel, page_count, entries.sh...  11.9 us
    all_to_all x1, blocking collectives, swap(): lax.all_to_all(shaped, 'req', split_axis=1, concat_axis=1, tiled=True)  6.67 us
    all_to_all x1, starting transfers between devices, exchange(): return lax.all_to_all(array, axis, split_axis=0, concat_axis=0, tiled=True)  6.35 us
    all_to_all x1, starting transfers between devices, swap(): lax.all_to_all(shaped, 'req', split_axis=1, concat_axis=1, tiled=True)  4.22 us
    dot_general x1, matrix products, feed_forward(): return jnp.dot(hidden, w_down, preferred_element_type=jnp.float32)  3.87 us
    dot_general x1, matrix products, on_device(): jnp.dot(attended, w_out, preferred_element_type=jnp.float32)  3.37 us
  transfers between devices with their start and end apart: 2, of which 2 were waited for; matrix products, arithmetic and copies ran while one was open for 2% of the time, Pallas kernels for 0%

profile of v1, /device:TPU:0, one launch (start us, length us, event | category | flops | bytes accessed | tf_op | source)
XLA Modules:
  0.0 154.9 jit_solution(12081766971337830890)
XLA Ops:
  0.0 0.9 reshape.206
  1.1 1.2 fusion.3
  3.1 4.2 %all-to-all-start = ((bf16[4,4,2,1536]{3,2,0,1:T(2,128)(2,1)}), bf16[4,4,2,1536]{3,2,0,1:T(2,128)(2,1)S(1)}, u32[]{:S(2)}, u32[]{:S(2)}) async-start(bf16[4,4,2,1536]{3,2,0,1:T(2,128)(2,1)} %copy.46), calls=%async_computation | async-start | bytes 196608 | tf_op jit(solution)/shard_map/all_to_all | solution.py:183
  8.3 0.8 constant_dynamic-slice_fusion
  9.4 2.2 %all-to-all-done = bf16[4,4,2,1536]{3,2,0,1:T(2,128)(2,1)S(1)} async-done(((bf16[4,4,2,1536]{3,2,0,1:T(2,128)(2,1)}), bf16[4,4,2,1536]{3,2,0,1:T(2,128)(2,1)S(1)}, u32[]{:S(2)}, u32[]{:S(2)}) %all-to-all-start) | async-done | bytes 98336 | tf_op jit(solution)/shard_map/all_to_all | solution.py:183
  12.4 3.3 %convolution_convert_fusion.5 = bf16[32,1536]{1,0:T(8,128)(2,1)S(1)} fusion(bf16[1536,1536]{1,0:T(8,128)(2,1)} %param.21, f32[4,1536,8]{1,2,0:T(8,128)S(1)} %get-tuple-element.21, f32[1536]{0:T(1024)S(1)} %copy-done.8, f32[32]{0:T(128)S(1)} %rsqrt.20), kind=kOutput, calls=%fused_computation.10 | convolution fusion | flops 151191552 | bytes 5019776 | tf_op jit(solution)/shard_map/dot_general | solution.py:227
  15.7 1.0 broadcast_in_dim.133
  16.7 6.3 %all-to-all-start.1 = ((bf16[8,32,1792]{2,1,0:T(8,128)(2,1)}), bf16[8,32,1792]{2,1,0:T(8,128)(2,1)S(1)}, u32[]{:S(2)}, u32[]{:S(2)}) async-start(bf16[8,32,1792]{2,1,0:T(8,128)(2,1)} %broadcast_in_dim.133), calls=%async_computation.1 | async-start | bytes 1835008 | tf_op jit(solution)/shard_map/all_to_all | solution.py:56
  25.0 21.0 %all-to-all-done.1 = bf16[8,32,1792]{2,1,0:T(8,128)(2,1)S(1)} async-done(((bf16[8,32,1792]{2,1,0:T(8,128)(2,1)}), bf16[8,32,1792]{2,1,0:T(8,128)(2,1)S(1)}, u32[]{:S(2)}, u32[]{:S(2)}) %all-to-all-start.1) | async-done | bytes 917536 | tf_op jit(solution)/shard_map/all_to_all | solution.py:56
  46.7 1.3 copy.49
  48.0 1.7 %reshape.211.refs_9_ = bf16[8,384,128]{2,1,0:T(8,128)(2,1)S(1)} reshape(bf16[8,8,4,1536]{3,2,1,0:T(4,128)(2,1)} %copy.49) | data formatting | bytes 1572864 | tf_op jit(solution)/shard_map/reshape | solution.py:232
  49.6 0.9 copy.64.refs_10_
  50.6 2.3 %copy-done.1 = bf16[72,128,256]{2,1,0:T(8,128)(2,1)S(1)} copy-done((bf16[72,128,256]{2,1,0:T(8,128)(2,1)S(1)}, bf16[72,128,256]{2,1,0:T(8,128)(2,1)}, u32[]{:S(2)}) %copy-start.1) | copy-done | bytes 4718616
  52.9 11.9 %shard_map.136 = bf16[8,384,128]{2,1,0:T(8,128)(2,1)S(1)} custom-call(s32[72]{0:T(128)S(1)} %reshape.209.table_ref, s32[8]{0:T(128)S(1)} %gather_fusion, bf16[72,128,256]{2,1,0:T(8,128)(2,1)S(1)} %copy-done.1, bf16[72,128,256]{2,1,0:T(8,128)(2,1)S(1)} %copy-done.1, bf16[72,128,256]{2,1,0:T(8,128)(2,1)S(1)} %copy-done.1, bf16[72,128,256]{2,1,0:T(8,128)(2,1)S(1)} %copy-done.1, ...), custom_call_target="tpu_custom_call" | custom-call | tf_op jit(solution)/shard_map/pallas_call | solution.py:124
  64.9 0.9 copy-done.2
  65.7 1.7 %reshape.215 = bf16[8,8,4,1536]{3,2,1,0:T(4,128)(2,1)S(1)} reshape(bf16[8,384,128]{2,1,0:T(8,128)(2,1)} %copy-done.2) | data formatting | bytes 1572864 | tf_op jit(solution)/shard_map/reshape | solution.py:237
  67.9 23.5 %all_to_all.30 = bf16[8,32,1536]{2,1,0:T(8,128)(2,1)S(1)} all-to-all(bf16[8,32,1536]{2,1,0:T(8,128)(2,1)S(1)} %bitcast.116), channel_id=1, replica_groups=mesh['req'=4,'kv'=8] {'kv'}, dimensions={0} | all-to-all | bytes 1572864 | tf_op jit(solution)/shard_map/all_to_all | solution.py:56
  91.5 3.4 %multiply_reduce_fusion = (f32[32]{0:T(128)S(1)}, f32[32,1536]{1,0:T(8,128)S(1)}) fusion(bf16[32,1536]{1,0:T(8,128)(2,1)S(1)} %reduce_sum.170, bf16[1536,1536]{1,0:T(8,128)(2,1)} %param.23, f32[4,1536,8]{1,2,0:T(8,128)S(1)} %copy-done.5), kind=kOutput, calls=%fused_computation.38 | convolution fusion | flops 151240672 | bytes 5210240 | tf_op jit(solution)/shard_map/dot_general | solution.py:243
  95.1 23.4 %all_to_all.31 = bf16[8,32,1536]{2,1,0:T(8,128)(2,1)S(1)} all-to-all(bf16[8,32,1536]{2,1,0:T(8,128)(2,1)S(1)} %broadcast_in_dim.147), channel_id=1, replica_groups=mesh['req'=4,'kv'=8] {'kv'}, dimensions={0} | all-to-all | bytes 1572864 | tf_op jit(solution)/shard_map/all_to_all | solution.py:56
  118.5 1.5 fusion.45
  119.9 3.9 %convolution_convert_fusion = bf16[256,1536]{1,0:T(8,128)(2,1)S(1)} fusion(bf16[576,1536]{1,0:T(8,128)(2,1)S(1)} %copy-done, bf16[256,1536]{1,0:T(8,128)(2,1)S(1)} %bitcast.118, bf16[1536,576]{0,1:T(8,128)(2,1)} %param.26, f32[256,576]{0,1:T(8,128)} %fusion.45), kind=kOutput, calls=%fused_computation.1 | convolution fusion | flops 907837440 | bytes 5701632 | tf_op jit(solution)/shard_map/dot_general | solution.py:29
  123.8 23.1 %all_to_all.32 = bf16[8,32,1536]{2,1,0:T(8,128)(2,1)S(1)} all-to-all(bf16[8,32,1536]{2,1,0:T(8,128)(2,1)S(1)} %bitcast.120), channel_id=1, replica_groups=mesh['req'=4,'kv'=8] {'kv'}, dimensions={0} | all-to-all | bytes 1572864 | tf_op jit(solution)/shard_map/all_to_all | solution.py:56
  147.2 6.7 %all_to_all.33 = bf16[4,4,2,1536]{3,2,0,1:T(2,128)(2,1)S(1)} all-to-all(bf16[4,4,2,1536]{3,2,0,1:T(2,128)(2,1)S(1)} %copy.58), channel_id=1, replica_groups=mesh['req'=4,'kv'=8] {'req'}, dimensions={1} | all-to-all | bytes 196608 | tf_op jit(solution)/shard_map/all_to_all | solution.py:183
  154.0 0.9 fusion.5
  (91 shorter events, 6.7 us)
Async XLA Ops:
  0.0 119.9 %copy-start = (bf16[576,1536]{1,0:T(8,128)(2,1)S(1)}, bf16[576,1536]{1,0:T(8,128)(2,1)}, u32[]{:S(2)}) copy-start(bf16[576,1536]{1,0:T(8,128)(2,1)} %param.27) | copy-start | bytes 5308420
  0.0 12.1 %copy-start.7 = (bf16[1536,256]{1,0:T(8,128)(2,1)S(1)}, bf16[1536,256]{1,0:T(8,128)(2,1)}, u32[]{:S(2)}) copy-start(bf16[1536,256]{1,0:T(8,128)(2,1)} %param.22) | copy-start | bytes 2359300
  0.0 12.1 %copy-start.8 = (f32[1536]{0:T(1024)S(1)}, f32[1536]{0:T(1024)}, u32[]{:S(2)}) copy-start(f32[1536]{0:T(1024)} %param.20) | copy-start | bytes 18436
  3.1 8.5 %all-to-all-start = ((bf16[4,4,2,1536]{3,2,0,1:T(2,128)(2,1)}), bf16[4,4,2,1536]{3,2,0,1:T(2,128)(2,1)S(1)}, u32[]{:S(2)}, u32[]{:S(2)}) async-start(bf16[4,4,2,1536]{3,2,0,1:T(2,128)(2,1)} %copy.46), calls=%async_computation | async-start | bytes 196608 | tf_op jit(solution)/shard_map/all_to_all | solution.py:183
  12.0 3.7 %copy-start.4 = (f32[4,1536,8]{1,2,0:T(8,128)}, f32[4,1536,8]{1,2,0:T(8,128)S(1)}, u32[]{:S(2)}) copy-start(f32[4,1536,8]{1,2,0:T(8,128)S(1)} %get-tuple-element.21) | copy-start | bytes 589828
  16.7 29.2 %all-to-all-start.1 = ((bf16[8,32,1792]{2,1,0:T(8,128)(2,1)}), bf16[8,32,1792]{2,1,0:T(8,128)(2,1)S(1)}, u32[]{:S(2)}, u32[]{:S(2)}) async-start(bf16[8,32,1792]{2,1,0:T(8,128)(2,1)} %broadcast_in_dim.133), calls=%async_computation.1 | async-start | bytes 1835008 | tf_op jit(solution)/shard_map/all_to_all | solution.py:56
  23.7 0.7 copy-start.3
  50.6 2.3 %copy-start.1 = (bf16[72,128,256]{2,1,0:T(8,128)(2,1)S(1)}, bf16[72,128,256]{2,1,0:T(8,128)(2,1)}, u32[]{:S(2)}) copy-start(bf16[72,128,256]{2,1,0:T(8,128)(2,1)} %refs_8_.1) | copy-start | bytes 14155780
  64.8 0.9 copy-start.2
  67.5 24.0 %copy-start.5 = (f32[4,1536,8]{1,2,0:T(8,128)S(1)}, f32[4,1536,8]{1,2,0:T(8,128)}, u32[]{:S(2)}) copy-start(f32[4,1536,8]{1,2,0:T(8,128)} %copy-done.4) | copy-start | bytes 589828
  91.5 3.4 %copy-start.9 = (f32[1536]{0:T(1024)S(1)}, f32[1536]{0:T(1024)}, u32[]{:S(2)}) copy-start(f32[1536]{0:T(1024)} %param.24) | copy-start | bytes 18436
  94.9 23.6 %copy-start.6 = (bf16[1536,576]{0,1:T(8,128)(2,1)S(1)}, bf16[1536,576]{0,1:T(8,128)(2,1)}, u32[]{:S(2)}) copy-start(bf16[1536,576]{0,1:T(8,128)(2,1)} %param.25) | copy-start | bytes 5308420

commit v2 on v1

--- a/solution.py
+++ b/solution.py
@@ -52,13 +52,296 @@
     return placed.reshape((BEAMS * halves,) + block.shape[1:])
 
 
-def exchange(array, axis):
-    return lax.all_to_all(array, axis, split_axis=0, concat_axis=0, tiled=True)
-
-
-def gathered(block, axis):
-    count = lax.axis_size(axis)
-    return exchange(jnp.broadcast_to(block[None], (count,) + block.shape), axis)
+MESH = pl.DeviceIdType.MESH
+
+
+class Sends:
+    def __init__(self, send_sem):
+        self.send_sem = send_sem
+        self.started = []
+
+    def go(self, where, source, target, arrived, peer):
+        copy = pltpu.make_async_remote_copy(
+            src_ref=source,
+            dst_ref=target,
+            send_sem=self.send_sem.at[len(self.started)],
+            recv_sem=arrived,
+            device_id={"kv": peer},
+            device_id_type=MESH,
+        )
+        self.started.append((where, copy))
+        if where is None:
+            copy.start()
+        else:
+            pl.when(where)(copy.start)
+
+    def finish(self):
+        for where, copy in self.started:
+            if where is None:
+                copy.wait_send()
+            else:
+                pl.when(where)(copy.wait_send)
+
+
+def landed(where, target, arrived):
+    def wait():
+        pltpu.make_async_copy(target, target, arrived).wait()
+
+    if where is None:
+        wait()
+    else:
+        pl.when(where)(wait)
+
+
+def place_on_lines(count):
+    me = lax.axis_index("kv")
+    low = lax.rem(me, 2)
+    high = me // 2
+    length = count // 2
+    above, below = high + 1 < length, high > 0
+    partner = high * 2 + 1 - low
+    up = jnp.minimum(high + 1, length - 1) * 2 + low
+    down = jnp.maximum(high - 1, 0) * 2 + low
+    return me, low, high, length, above, below, partner, up, down
+
+
+def greet(above, below, partner, up, down):
+    barrier = pltpu.get_barrier_semaphore()
+
+    def hello(peer):
+        pl.semaphore_signal(barrier, inc=1, device_id={"kv": peer}, device_id_type=MESH)
+
+    hello(partner)
+    pl.when(above)(lambda: hello(up))
+    pl.when(below)(lambda: hello(down))
+    pl.semaphore_wait(barrier, 1 + above.astype(jnp.int32) + below.astype(jnp.int32))
+
+
+def gather_kernel(count, own_ref, all_ref, send_sem, first_sem, second_sem):
+    me, low, high, length, above, below, partner, up, down = place_on_lines(count)
+    middle = own_ref.shape[0] // 2
+    first, second = pl.ds(0, middle), pl.ds(middle, middle)
+    greet(above, below, partner, up, down)
+    sends = Sends(send_sem)
+
+    def spread(where, block, source, part, sems, peer):
+        sends.go(where, source, all_ref.at[block, part], sems.at[block], peer)
+
+    spread(None, me, own_ref.at[second], second, second_sem, partner)
+    for where, peer in ((above, up), (below, down)):
+        spread(where, me, own_ref.at[first], first, first_sem, peer)
+        spread(where, me, own_ref.at[second], second, second_sem, peer)
+    spread(None, me, own_ref.at[first], first, first_sem, partner)
+    all_ref[me] = own_ref[...]
+    landed(None, all_ref.at[partner, second], second_sem.at[partner])
+    for where, peer in ((above, up), (below, down)):
+        spread(where, partner, all_ref.at[partner, second], second, second_sem, peer)
+    for distance in range(1, length):
+        for source, here, where, peer in (
+            (jnp.maximum(high - distance, 0), high >= distance, above, up),
+            (jnp.minimum(high + distance, length - 1), high + distance < length, below, down),
+        ):
+            same = source * 2 + low
+            cross = source * 2 + 1 - low
+            onward = here & where
+            landed(here, all_ref.at[same, first], first_sem.at[same])
+            spread(onward, same, all_ref.at[same, first], first, first_sem, peer)
+            spread(here, same, all_ref.at[same, first], first, first_sem, partner)
+            landed(here, all_ref.at[same, second], second_sem.at[same])
+            spread(onward, same, all_ref.at[same, second], second, second_sem, peer)
+            landed(here, all_ref.at[cross, second], second_sem.at[cross])
+            spread(onward, cross, all_ref.at[cross, second], second, second_sem, peer)
+    for line in range(length):
+        cross = line * 2 + 1 - low
+        landed(None, all_ref.at[cross, first], first_sem.at[cross])
+    sends.finish()
+
+
+def gathered(block, count, collective_id):
+    whole = pl.BlockSpec(memory_space=pltpu.VMEM)
+    return pl.pallas_call(
+        functools.partial(gather_kernel, count),
+        out_shape=jax.ShapeDtypeStruct((count,) + block.shape, block.dtype),
+        in_specs=[whole],
+        out_specs=whole,
+        scratch_shapes=[
+            pltpu.SemaphoreType.DMA((8 + 10 * (count // 2),)),
+            pltpu.SemaphoreType.DMA((count,)),
+            pltpu.SemaphoreType.DMA((count,)),
+        ],
+        compiler_params=pltpu.CompilerParams(
+            collective_id=collective_id, has_side_effects=True, vmem_limit_bytes=40 * 2**20
+        ),
+    )(block)
+
+
+def reduce_kernel(
+    count,
+    terms_ref,
+    sum_ref,
+    cross_first,
+    up_first,
+    down_first,
+    stage_first,
+    cross_second,
+    up_second,
+    down_second,
+    stage_second,
+    stage_cross,
+    send_sem,
+    cross_sem,
+    up_sem,
+    down_sem,
+):
+    me, low, high, length, above, below, partner, up, down = place_on_lines(count)
+    middle = sum_ref.shape[0] // 2
+    first, second = pl.ds(0, middle), pl.ds(middle, middle)
+    greet(above, below, partner, up, down)
+    sends = Sends(send_sem)
+    for line in range(length):
+        sends.go(
+            None,
+            terms_ref.at[line * 2 + 1 - low, first],
+            cross_first.at[line],
+            cross_sem.at[line],
+            partner,
+        )
+
+    def wide(ref):
+        return ref[...].astype(jnp.float32)
+
+    def base_first(line):
+        return wide(terms_ref.at[line * 2 + low, first]) + wide(cross_first.at[line])
+
+    def pass_on(here, line, behind, slot, stage, arrived, ahead, base):
+        def with_slot():
+            stage[...] = (base() + wide(slot)).astype(stage.dtype)
+
+        def alone():
+            stage[...] = base().astype(stage.dtype)
+
+        landed(here & behind, slot, arrived)
+        pl.when(here & behind)(with_slot)
+        pl.when(here & jnp.logical_not(behind))(alone)
+        sends.go(here, stage, slot, arrived, ahead)
+
+    directions = (
+        (1, below, up_second, up_first, up_sem, up),
+        (-1, above, down_second, down_first, down_sem, down),
+    )
+    for distance in range(length - 1, 0, -1):
+        for sign, behind, slot, _, sems, ahead in directions:
+            line = high + sign * distance
+            here = (line < length) & (line >= 0)
+            line = jnp.clip(line, 0, length - 1)
+            for other in range(2):
+                side = low if other == 0 else 1 - low
+                block = line * 2 + side
+                pass_on(
+                    here,
+                    line,
+                    behind,
+                    slot.at[block],
+                    stage_second.at[block],
+                    sems.at[length + block],
+                    ahead,
+                    lambda block=block: wide(terms_ref.at[block, second]),
+                )
+    for line in range(length):
+        landed(None, cross_first.at[line], cross_sem.at[line])
+    for distance in range(length - 1, 0, -1):
+        for sign, behind, _, slot, sems, ahead in directions:
+            line = high + sign * distance
+            here = (line < length) & (line >= 0)
+            line = jnp.clip(line, 0, length - 1)
+            pass_on(
+                here,
+                line,
+                behind,
+                slot.at[line],
+                stage_first.at[line],
+                sems.at[line],
+                ahead,
+                lambda line=line: base_first(line),
+            )
+
+    def collect(into, part, value, up_slot, down_slot, up_arrived, down_arrived):
+        into[part, :] = value
+        landed(below, up_slot, up_arrived)
+        landed(above, down_slot, down_arrived)
+
+        def add(slot):
+            into[part, :] += wide(slot)
+
+        pl.when(below)(lambda: add(up_slot))
+        pl.when(above)(lambda: add(down_slot))
+
+    collect(
+        sum_ref,
+        second,
+        wide(terms_ref.at[partner, second]),
+        up_second.at[partner],
+        down_second.at[partner],
+        up_sem.at[length + partner],
+        down_sem.at[length + partner],
+    )
+    stage_cross[...] = sum_ref[second, :].astype(stage_cross.dtype)
+    sends.go(None, stage_cross, cross_second, cross_sem.at[length], partner)
+    collect(
+        sum_ref,
+        second,
+        wide(terms_ref.at[me, second]),
+        up_second.at[me],
+        down_second.at[me],
+        up_sem.at[length + me],
+        down_sem.at[length + me],
+    )
+    collect(
+        sum_ref,
+        first,
+        base_first(high),
+        up_first.at[high],
+        down_first.at[high],
+        up_sem.at[high],
+        down_sem.at[high],
+    )
+    landed(None, cross_second, cross_sem.at[length])
+    sum_ref[second, :] += wide(cross_second)
+    sends.finish()
+
+
+def reduced(terms, collective_id):
+    count, rows, width = terms.shape
+    length = count // 2
+    whole = pl.BlockSpec(memory_space=pltpu.VMEM)
+
+    def slots(*shape):
+        return pltpu.VMEM(shape + (rows // 2, width), terms.dtype)
+
+    return pl.pallas_call(
+        functools.partial(reduce_kernel, count),
+        out_shape=jax.ShapeDtypeStruct((rows, width), jnp.float32),
+        in_specs=[whole],
+        out_specs=whole,
+        scratch_shapes=[
+            slots(length),
+            slots(length),
+            slots(length),
+            slots(length),
+            slots(),
+            slots(count),
+            slots(count),
+            slots(count),
+            slots(),
+            pltpu.SemaphoreType.DMA((8 * length,)),
+            pltpu.SemaphoreType.DMA((length + 1,)),
+            pltpu.SemaphoreType.DMA((length + count,)),
+            pltpu.SemaphoreType.DMA((length + count,)),
+        ],
+        compiler_params=pltpu.CompilerParams(
+            collective_id=collective_id, has_side_effects=True, vmem_limit_bytes=40 * 2**20
+        ),
+    )(terms)
 
 
 def reordered(selector, array):
@@ -227,7 +510,7 @@
     query = jnp.dot(normed, w_query, preferred_element_type=jnp.float32).astype(jnp.bfloat16)
     fresh = jnp.dot(normed, w_keyval, preferred_element_type=jnp.float32).astype(jnp.bfloat16)
     sent = jnp.concatenate([query, fresh], axis=1)
-    shared = pick_half(gathered(sent, "kv"), halves, half)
+    shared = pick_half(gathered(sent, kv_count, 1), halves, half)
     shared = shared.reshape(BEAMS, steps, rows, -1).transpose(2, 0, 1, 3)
     queries = shared[..., : heads * head_dim].reshape(rows, BEAMS * steps * heads, head_dim)
     entries = shared[..., heads * head_dim :].reshape(rows, BEAMS * steps, 2 * head_dim)
@@ -235,17 +518,15 @@
         table - device * pool.shape[0], length, pool, queries, entries, marks
     )
     answers = answers.reshape(rows, BEAMS, steps, heads * head_dim).transpose(1, 2, 0, 3)
-    returned = exchange(
-        place_block(answers.reshape(BEAMS, steps * rows, heads * head_dim), halves, half), "kv"
-    )
-    attended = jnp.sum(returned.astype(jnp.float32), axis=0).astype(jnp.bfloat16)
+    attended = reduced(
+        place_block(answers.reshape(BEAMS, steps * rows, heads * head_dim), halves, half), 2
+    ).astype(jnp.bfloat16)
     residual = (
         current.astype(jnp.float32) + jnp.dot(attended, w_out, preferred_element_type=jnp.float32)
     ).astype(jnp.bfloat16)
-    everyone = gathered(rms_round(residual, norm_mlp), "kv").reshape(-1, width)
+    everyone = gathered(rms_round(residual, norm_mlp), kv_count, 3).reshape(-1, width)
     terms = feed_forward(everyone, w_gate, w_up, w_down).astype(jnp.bfloat16)
-    terms = exchange(terms.reshape(kv_count, steps * rows, width), "kv")
-    summed = jnp.sum(terms.astype(jnp.float32), axis=0)
+    summed = reduced(terms.reshape(kv_count, steps * rows, width), 4)
     finished = (residual.astype(jnp.float32) + summed).astype(jnp.bfloat16)
     finished = finished.reshape(steps, rows, width)
     return reordered(by_target, swap(reordered(by_anchor.T, finished)))

time: 156 us -> 132 us (0.85)
  Pallas kernels: 11.9 us -> 82.1 us
  blocking collectives: 76.5 us -> 7.12 us
  waiting for transfers between devices: 23.1 us -> 0.01 us
  starting transfers between devices: 10.6 us -> 4.21 us
  local copies, waits for them, and re-layouts: 15.5 us -> 18.1 us
  matrix products: 14.8 us -> 16.5 us
    pallas_call x0 -> x4, Pallas kernels: none -> 70.2 us  [the longest x2 37.9 us: gathered(): pl.pallas_call(functools.partial(gather_kernel, count), out_shape=jax.Sha...]
    all_to_all x3 -> x0, blocking collectives: 69.9 us -> none  [exchange(): return lax.all_to_all(array, axis, split_axis=0, concat_axis=0, tiled=True)]
    all_to_all x1 -> x0, waiting for transfers between devices: 21 us -> none  [exchange(): return lax.all_to_all(array, axis, split_axis=0, concat_axis=0, tiled=True)]
    all_to_all x1 -> x0, starting transfers between devices: 6.35 us -> none  [exchange(): return lax.all_to_all(array, axis, split_axis=0, concat_axis=0, tiled=True)]
    all_to_all x1, waiting for transfers between devices: 2.17 us -> 0.01 us  [swap(): lax.all_to_all(shaped, 'req', split_axis=1, concat_axis=1, tiled=True)]
    unnamed x28 -> x34, local copies, waits for them, and re-layouts: 3.27 us -> 3.28 us
  transfers between devices with their start and end apart: 2 -> 1, of which waited for: 2 -> 0; matrix products, arithmetic and copies ran while one was open for 2% -> 3% of each run, Pallas kernels for 0% -> 0%
where the time goes in v2:
time: 132 us; the launch traced here: 131 us
  Pallas kernels  82.1 us (62%)
  local copies, waits for them, and re-layouts  18.1 us (14%)
  matrix products  16.5 us (12%)
  blocking collectives  7.12 us (5%)
  starting transfers between devices  4.21 us (3%)
  other arithmetic  2.95 us (2%)
    pallas_call x2, Pallas kernels, gathered(): pl.pallas_call(functools.partial(gather_kernel, count), out_shape=jax.Sha...  37.9 us
    pallas_call x2, Pallas kernels, reduced(): pl.pallas_call(functools.partial(reduce_kernel, count), out_shape=jax.Sha...  32.2 us
    pallas_call x1, Pallas kernels, attend(): pl.pallas_call(functools.partial(attention_kernel, page_count, entries.sh...  11.9 us
    all_to_all x1, blocking collectives, swap(): lax.all_to_all(shaped, 'req', split_axis=1, concat_axis=1, tiled=True)  7.12 us
    all_to_all x1, starting transfers between devices, swap(): lax.all_to_all(shaped, 'req', split_axis=1, concat_axis=1, tiled=True)  4.21 us
    dot_general x1, matrix products, feed_forward(): return jnp.dot(hidden, w_down, preferred_element_type=jnp.float32)  3.87 us
    dot_general x1, matrix products, on_device(): jnp.dot(attended, w_out, preferred_element_type=jnp.float32)  3.48 us
    dot_general x4, matrix products, reordered(): jnp.einsum('pi,tiw->tpw', selector.astype(jnp.bfloat16), array, preferred...  3.39 us
  transfers between devices with their start and end apart: 1, of which 0 were waited for; matrix products, arithmetic and copies ran while one was open for 3% of the time, Pallas kernels for 0%

profile of v2, /device:TPU:0, one launch (start us, length us, event | category | flops | bytes accessed | tf_op | source)
XLA Modules:
  0.0 131.5 jit_solution(1473605784584681601)
XLA Ops:
  0.0 0.9 reshape.204
  1.1 1.2 fusion.3
  3.0 4.2 %all-to-all-start = ((bf16[4,4,2,1536]{3,2,0,1:T(2,128)(2,1)}), bf16[4,4,2,1536]{3,2,0,1:T(2,128)(2,1)S(1)}, u32[]{:S(2)}, u32[]{:S(2)}) async-start(bf16[4,4,2,1536]{3,2,0,1:T(2,128)(2,1)} %copy.46), calls=%async_computation | async-start | bytes 196608 | tf_op jit(solution)/shard_map/all_to_all | solution.py:466
  12.6 1.6 %reshape.206 = bf16[4,8,1536]{2,1,0:T(8,128)(2,1)} reshape(bf16[4,4,2,1536]{3,2,1,0:T(2,128)(2,1)} %copy.47) | data formatting | bytes 196608 | tf_op jit(solution)/shard_map/reshape | solution.py:466
  14.2 1.2 multiply_reduce_fusion.1
  16.0 1.3 %rsqrt.20 = f32[32]{0:T(128)} reshape(f32[4,8]{1,0:T(4,128)} %add_rsqrt_fusion) | data formatting | bytes 256 | tf_op jit(solution)/shard_map/rsqrt | solution.py:22
  17.4 0.9 convolution_convert_fusion.6
  18.3 3.3 %convolution_convert_fusion.5 = bf16[32,1536]{1,0:T(8,128)(2,1)S(1)} fusion(bf16[1536,1536]{1,0:T(8,128)(2,1)} %param.21, f32[4,1536,8]{1,2,0:T(8,128)S(1)} %get-tuple-element.21, f32[1536]{0:T(1024)S(1)} %copy-done.8, f32[32]{0:T(128)} %rsqrt.20), kind=kOutput, calls=%fused_computation.10 | convolution fusion | flops 151191552 | bytes 5019776 | tf_op jit(solution)/shard_map/dot_general | solution.py:510
  21.6 20.4 %shard_map.136 = bf16[8,32,1792]{2,1,0:T(8,128)(2,1)S(1)} custom-call(bf16[32,1792]{1,0:T(8,128)(2,1)S(1)} %pad_maximum_fusion.1.own_ref), custom_call_target="tpu_custom_call" | custom-call | tf_op jit(solution)/shard_map/pallas_call | solution.py:162
  42.4 1.2 slice.34
  44.3 1.7 %reshape.209.refs_9_ = bf16[8,384,128]{2,1,0:T(8,128)(2,1)S(1)} reshape(bf16[8,8,4,1536]{3,2,1,0:T(4,128)(2,1)} %slice.34) | data formatting | bytes 1572864 | tf_op jit(solution)/shard_map/reshape | solution.py:515
  46.0 0.9 reshape.210.refs_10_
  46.9 2.3 %copy-done.1 = bf16[72,128,256]{2,1,0:T(8,128)(2,1)S(1)} copy-done((bf16[72,128,256]{2,1,0:T(8,128)(2,1)S(1)}, bf16[72,128,256]{2,1,0:T(8,128)(2,1)}, u32[]{:S(2)}) %copy-start.1) | copy-done | bytes 4718616
  49.2 11.9 %shard_map.137 = bf16[8,384,128]{2,1,0:T(8,128)(2,1)S(1)} custom-call(s32[72]{0:T(128)S(1)} %reshape.207.table_ref, s32[8]{0:T(128)S(1)} %gather_fusion, bf16[72,128,256]{2,1,0:T(8,128)(2,1)S(1)} %copy-done.1, bf16[72,128,256]{2,1,0:T(8,128)(2,1)S(1)} %copy-done.1, bf16[72,128,256]{2,1,0:T(8,128)(2,1)S(1)} %copy-done.1, bf16[72,128,256]{2,1,0:T(8,128)(2,1)S(1)} %copy-done.1, ...), custom_call_target="tpu_custom_call" | custom-call | tf_op jit(solution)/shard_map/pallas_call | solution.py:407
  61.1 0.9 copy-done.2
  62.0 1.8 %reshape.213 = bf16[8,8,4,1536]{3,2,1,0:T(4,128)(2,1)S(1)} reshape(bf16[8,384,128]{2,1,0:T(8,128)(2,1)} %copy-done.2) | data formatting | bytes 1572864 | tf_op jit(solution)/shard_map/reshape | solution.py:520
  64.2 16.5 %shard_map.138 = f32[32,1536]{1,0:T(8,128)S(1)} custom-call(bf16[8,32,1536]{2,1,0:T(8,128)(2,1)S(1)} %bitcast.115), custom_call_target="tpu_custom_call" | custom-call | tf_op jit(solution)/shard_map/pallas_call | solution.py:321
  80.8 3.5 %multiply_reduce_fusion = (f32[32]{0:T(128)S(1)}, f32[32,1536]{1,0:T(8,128)S(1)}) fusion(bf16[1536,1536]{1,0:T(8,128)(2,1)} %param.23, f32[32,1536]{1,0:T(8,128)S(1)} %shard_map.138, f32[4,1536,8]{1,2,0:T(8,128)S(1)} %copy-done.5), kind=kOutput, calls=%fused_computation.38 | convolution fusion | flops 151289824 | bytes 5308544 | tf_op jit(solution)/shard_map/dot_general | solution.py:525
  84.4 17.5 %shard_map.139 = bf16[8,32,1536]{2,1,0:T(8,128)(2,1)S(1)} custom-call(bf16[32,1536]{1,0:T(8,128)(2,1)S(1)} %multiply_convert_fusion.own_ref), custom_call_target="tpu_custom_call" | custom-call | tf_op jit(solution)/shard_map/pallas_call | solution.py:162
  101.9 1.5 %fusion.46 = f32[256,576]{0,1:T(8,128)} fusion(bf16[256,1536]{1,0:T(8,128)(2,1)S(1)} %bitcast.113, bf16[1536,576]{0,1:T(8,128)(2,1)S(1)} %copy-done.6), kind=kOutput, calls=%fused_computation.118 | convolution fusion | flops 452984832 | bytes 3145728 | tf_op jit(solution)/shard_map/dot_general | solution.py:26
  103.4 3.9 %convolution_convert_fusion = bf16[256,1536]{1,0:T(8,128)(2,1)S(1)} fusion(bf16[576,1536]{1,0:T(8,128)(2,1)S(1)} %copy-done, bf16[256,1536]{1,0:T(8,128)(2,1)S(1)} %bitcast.114, bf16[1536,576]{0,1:T(8,128)(2,1)} %param.26, f32[256,576]{0,1:T(8,128)} %fusion.46), kind=kOutput, calls=%fused_computation.1 | convolution fusion | flops 907837440 | bytes 5701632 | tf_op jit(solution)/shard_map/dot_general | solution.py:29
  107.3 15.7 %shard_map.140 = f32[32,1536]{1,0:T(8,128)S(1)} custom-call(bf16[8,32,1536]{2,1,0:T(8,128)(2,1)S(1)} %bitcast.116), custom_call_target="tpu_custom_call" | custom-call | tf_op jit(solution)/shard_map/pallas_call | solution.py:321
  123.4 7.1 %all_to_all.10 = bf16[4,4,2,1536]{3,2,0,1:T(2,128)(2,1)S(1)} all-to-all(bf16[4,4,2,1536]{3,2,0,1:T(2,128)(2,1)S(1)} %copy.57), channel_id=1, replica_groups=mesh['req'=4,'kv'=8] {'req'}, dimensions={1} | all-to-all | bytes 196608 | tf_op jit(solution)/shard_map/all_to_all | solution.py:466
  130.6 0.9 fusion.5
  (92 shorter events, 8.7 us)
Async XLA Ops:
  0.0 103.4 %copy-start = (bf16[576,1536]{1,0:T(8,128)(2,1)S(1)}, bf16[576,1536]{1,0:T(8,128)(2,1)}, u32[]{:S(2)}) copy-start(bf16[576,1536]{1,0:T(8,128)(2,1)} %param.27) | copy-start | bytes 5308420
  1.1 9.4 %copy-start.11 = (s32[8]{0:T(128)}, s32[8]{0:T(128)S(1)}, u32[]{:S(2)}) copy-start(s32[8]{0:T(128)S(1)} %multiply_add_fusion.1) | copy-start | bytes 100
  3.0 8.9 %all-to-all-start = ((bf16[4,4,2,1536]{3,2,0,1:T(2,128)(2,1)}), bf16[4,4,2,1536]{3,2,0,1:T(2,128)(2,1)S(1)}, u32[]{:S(2)}, u32[]{:S(2)}) async-start(bf16[4,4,2,1536]{3,2,0,1:T(2,128)(2,1)} %copy.46), calls=%async_computation | async-start | bytes 196608 | tf_op jit(solution)/shard_map/all_to_all | solution.py:466
  10.6 0.7 copy-start.3
  11.0 6.4 %copy-start.7 = (bf16[1536,256]{1,0:T(8,128)(2,1)S(1)}, bf16[1536,256]{1,0:T(8,128)(2,1)}, u32[]{:S(2)}) copy-start(bf16[1536,256]{1,0:T(8,128)(2,1)} %param.22) | copy-start | bytes 2359300
  11.0 6.4 %copy-start.8 = (f32[1536]{0:T(1024)S(1)}, f32[1536]{0:T(1024)}, u32[]{:S(2)}) copy-start(f32[1536]{0:T(1024)} %param.20) | copy-start | bytes 18436
  15.4 6.2 %copy-start.4 = (f32[4,1536,8]{1,2,0:T(8,128)}, f32[4,1536,8]{1,2,0:T(8,128)S(1)}, u32[]{:S(2)}) copy-start(f32[4,1536,8]{1,2,0:T(8,128)S(1)} %get-tuple-element.21) | copy-start | bytes 589828
  46.9 2.3 %copy-start.1 = (bf16[72,128,256]{2,1,0:T(8,128)(2,1)S(1)}, bf16[72,128,256]{2,1,0:T(8,128)(2,1)}, u32[]{:S(2)}) copy-start(bf16[72,128,256]{2,1,0:T(8,128)(2,1)} %refs_8_.1) | copy-start | bytes 14155780
  61.1 0.9 copy-start.2
  62.0 18.8 %copy-start.5 = (f32[4,1536,8]{1,2,0:T(8,128)S(1)}, f32[4,1536,8]{1,2,0:T(8,128)}, u32[]{:S(2)}) copy-start(f32[4,1536,8]{1,2,0:T(8,128)} %copy-done.4) | copy-start | bytes 589828
  80.8 3.5 %copy-start.9 = (f32[1536]{0:T(1024)S(1)}, f32[1536]{0:T(1024)}, u32[]{:S(2)}) copy-start(f32[1536]{0:T(1024)} %param.24) | copy-start | bytes 18436
  80.8 21.2 %copy-start.6 = (bf16[1536,576]{0,1:T(8,128)(2,1)S(1)}, bf16[1536,576]{0,1:T(8,128)(2,1)}, u32[]{:S(2)}) copy-start(bf16[1536,576]{0,1:T(8,128)(2,1)} %param.25) | copy-start | bytes 5308420
  103.4 19.6 %copy-start.10 = (s32[8]{0:T(128)S(1)}, s32[8]{0:T(128)}, u32[]{:S(2)}) copy-start(s32[8]{0:T(128)} %multiply_add_fusion) | copy-start | bytes 100
  107.3 23.3 %copy-start.12 = (s32[8]{0:T(128)S(1)}, s32[8]{0:T(128)}, u32[]{:S(2)}) copy-start(s32[8]{0:T(128)} %copy-done.11) | copy-start | bytes 100

commit v3 on v2

--- a/solution.py
+++ b/solution.py
@@ -117,11 +117,12 @@
     pl.semaphore_wait(barrier, 1 + above.astype(jnp.int32) + below.astype(jnp.int32))
 
 
-def gather_kernel(count, own_ref, all_ref, send_sem, first_sem, second_sem):
+def gather_kernel(count, greeting, own_ref, all_ref, send_sem, first_sem, second_sem):
     me, low, high, length, above, below, partner, up, down = place_on_lines(count)
     middle = own_ref.shape[0] // 2
     first, second = pl.ds(0, middle), pl.ds(middle, middle)
-    greet(above, below, partner, up, down)
+    if greeting:
+        greet(above, below, partner, up, down)
     sends = Sends(send_sem)
 
     def spread(where, block, source, part, sems, peer):
@@ -160,15 +161,11 @@
 def gathered(block, count, collective_id):
     whole = pl.BlockSpec(memory_space=pltpu.VMEM)
     return pl.pallas_call(
-        functools.partial(gather_kernel, count),
+        functools.partial(gather_kernel, count, True),
         out_shape=jax.ShapeDtypeStruct((count,) + block.shape, block.dtype),
         in_specs=[whole],
         out_specs=whole,
-        scratch_shapes=[
-            pltpu.SemaphoreType.DMA((8 + 10 * (count // 2),)),
-            pltpu.SemaphoreType.DMA((count,)),
-            pltpu.SemaphoreType.DMA((count,)),
-        ],
+        scratch_shapes=gather_semaphores(count),
         compiler_params=pltpu.CompilerParams(
             collective_id=collective_id, has_side_effects=True, vmem_limit_bytes=40 * 2**20
         ),
@@ -310,56 +307,112 @@
     sends.finish()
 
 
+def gather_semaphores(count):
+    return [
+        pltpu.SemaphoreType.DMA((8 + 10 * (count // 2),)),
+        pltpu.SemaphoreType.DMA((count,)),
+        pltpu.SemaphoreType.DMA((count,)),
+    ]
+
+
+def reduce_scratch(terms):
+    count, rows, width = terms.shape
+    length = count // 2
+
+    def slots(*shape):
+        return pltpu.VMEM(shape + (rows // 2, width), terms.dtype)
+
+    return [
+        slots(length),
+        slots(length),
+        slots(length),
+        slots(length),
+        slots(),
+        slots(count),
+        slots(count),
+        slots(count),
+        slots(),
+        pltpu.SemaphoreType.DMA((8 * length,)),
+        pltpu.SemaphoreType.DMA((length + 1,)),
+        pltpu.SemaphoreType.DMA((length + count,)),
+        pltpu.SemaphoreType.DMA((length + count,)),
+    ]
+
+
 def reduced(terms, collective_id):
     count, rows, width = terms.shape
-    length = count // 2
     whole = pl.BlockSpec(memory_space=pltpu.VMEM)
-
-    def slots(*shape):
-        return pltpu.VMEM(shape + (rows // 2, width), terms.dtype)
-
     return pl.pallas_call(
         functools.partial(reduce_kernel, count),
         out_shape=jax.ShapeDtypeStruct((rows, width), jnp.float32),
         in_specs=[whole],
         out_specs=whole,
-        scratch_shapes=[
-            slots(length),
-            slots(length),
-            slots(length),
-            slots(length),
-            slots(),
-            slots(count),
-            slots(count),
-            slots(count),
-            slots(),
-            pltpu.SemaphoreType.DMA((8 * length,)),
-            pltpu.SemaphoreType.DMA((length + 1,)),
-            pltpu.SemaphoreType.DMA((length + count,)),
-            pltpu.SemaphoreType.DMA((length + count,)),
-        ],
+        scratch_shapes=reduce_scratch(terms),
         compiler_params=pltpu.CompilerParams(
             collective_id=collective_id, has_side_effects=True, vmem_limit_bytes=40 * 2**20
         ),
     )(terms)
 
 
+def share_kernel(count, terms_ref, all_ref, sum_ref, own_ref, *scratch):
+    reduce_kernel(count, terms_ref, sum_ref, *scratch[:-3])
+    own_ref[...] = sum_ref[...].astype(own_ref.dtype)
+    gather_kernel(count, False, own_ref, all_ref, *scratch[-3:])
+
+
+def shared_sum(terms, collective_id):
+    count, rows, width = terms.shape
+    whole = pl.BlockSpec(memory_space=pltpu.VMEM)
+    return pl.pallas_call(
+        functools.partial(share_kernel, count),
+        out_shape=jax.ShapeDtypeStruct(terms.shape, terms.dtype),
+        in_specs=[whole],
+        out_specs=whole,
+        scratch_shapes=[
+            pltpu.VMEM((rows, width), jnp.float32),
+            pltpu.VMEM((rows, width), terms.dtype),
+        ]
+        + reduce_scratch(terms)
+        + gather_semaphores(count),
+        compiler_params=pltpu.CompilerParams(
+            collective_id=collective_id, has_side_effects=True, vmem_limit_bytes=40 * 2**20
+        ),
+    )(terms)
+
+
 def reordered(selector, array):
     return jnp.einsum(
         "pi,tiw->tpw", selector.astype(jnp.bfloat16), array, preferred_element_type=jnp.float32
     ).astype(jnp.bfloat16)
 
 
-def attention_kernel(page_count, entries, table_ref, length_ref, *refs):
+def attention_kernel(page_count, heads, stride, table_ref, length_ref, *refs):
     pages = refs[:page_count]
-    q_ref, new_ref, mask_ref, out_ref = refs[page_count:]
+    q_ref, new_ref, mask_ref, out_ref, q_heads, new_parts, out_heads = refs[page_count:]
     row = pl.program_id(0)
     length = length_ref[row]
-    head_dim = q_ref.shape[-1]
+    entries = mask_ref.shape[1]
+    head_dim = q_ref.shape[1] // heads
     span = page_count * PAGE
-    queries = q_ref[0]
-    marks = mask_ref[0].astype(jnp.float32)
-    bias = marks[:, :entries]
+    family = pl.ds(row, entries, stride=stride)
+
+    def columns(part):
+        return pl.ds(part * head_dim, head_dim)
+
+    @pl.when(row == 0)
+    def spread():
+        for head in range(heads):
+            q_heads[head] = q_ref[:, columns(head)].astype(jnp.float32)
+        for part in range(2):
+            new_parts[part] = new_ref[:, columns(part)].astype(jnp.float32)
+
+    queries = jnp.concatenate(
+        [q_heads[head, family, :] for head in range(heads)], axis=0
+    ).astype(jnp.bfloat16)
+    new_keys = new_parts[0, family, :].astype(jnp.bfloat16)
+    new_values = new_parts[1, family, :].astype(jnp.bfloat16)
+    marks = jnp.concatenate([mask_ref[0]] * heads, axis=0)
+    linked = marks[:, :entries]
     held = marks[:, entries : entries + 1]
     step = marks[:, entries + 1 : entries + 2].astype(jnp.int32)
     keys = jnp.concatenate([page[0, :, :head_dim] for page in pages], axis=0)
@@ -371,12 +424,9 @@
     scores = lax.dot_general(queries, keys, contract, preferred_element_type=jnp.float32) * scale
     scores = jnp.where((shifted < WINDOW) & (shifted > step), scores, NEGATIVE)
     fresh = (
-        lax.dot_general(
-            queries, new_ref[0, :, :head_dim], contract, preferred_element_type=jnp.float32
-        )
-        * scale
-    )
-    fresh = jnp.where(bias > 0.5, fresh, NEGATIVE)
+        lax.dot_general(queries, new_keys, contract, preferred_element_type=jnp.float32) * scale
+    )
+    fresh = jnp.where(linked > 0.5, fresh, NEGATIVE)
     highest = jnp.maximum(
         jnp.max(scores, axis=-1, keepdims=True), jnp.max(fresh, axis=-1, keepdims=True)
     )
@@ -386,14 +436,22 @@
         fresh_weights.astype(jnp.float32), axis=-1, keepdims=True
     )
     weighted = jnp.dot(weights, values, preferred_element_type=jnp.float32) + jnp.dot(
-        fresh_weights, new_ref[0, :, head_dim:], preferred_element_type=jnp.float32
-    )
-    out_ref[0] = jnp.where(held > 0.5, weighted / totals, 0.0).astype(jnp.bfloat16)
+        fresh_weights, new_values, preferred_element_type=jnp.float32
+    )
+    answers = jnp.where(held > 0.5, weighted / totals, 0.0)
+    for head in range(heads):
+        out_heads[head, family, :] = answers[head * entries : (head + 1) * entries]
+
+    @pl.when(row == pl.num_programs(0) - 1)
+    def gather_heads():
+        for head in range(heads):
+            out_ref[:, columns(head)] = out_heads[head].astype(out_ref.dtype)
 
 
 def attend(local_table, length, pool, queries, entries, marks):
-    rows, count, head_dim = queries.shape
-    page_count = local_table.shape[1]
+    head_dim = pool.shape[2] // 2
+    rows, page_count = local_table.shape
+    heads = queries.shape[1] // head_dim
 
     def page_spec(index):
         return pl.BlockSpec(
@@ -401,20 +459,30 @@
             lambda row, table_ref, length_ref: (table_ref[row * page_count + index], 0, 0),
         )
 
-    def row_spec(shape):
-        return pl.BlockSpec((1,) + shape[1:], lambda row, table_ref, length_ref: (row, 0, 0))
+    def whole(array):
+        return pl.BlockSpec(array.shape, lambda row, table_ref, length_ref: (0, 0))
 
     return pl.pallas_call(
-        functools.partial(attention_kernel, page_count, entries.shape[1]),
-        out_shape=jax.ShapeDtypeStruct((rows, count, head_dim), jnp.bfloat16),
+        functools.partial(attention_kernel, page_count, heads, rows),
+        out_shape=jax.ShapeDtypeStruct(queries.shape, queries.dtype),
         grid_spec=pltpu.PrefetchScalarGridSpec(
             num_scalar_prefetch=2,
             grid=(rows,),
             in_specs=[page_spec(index) for index in range(page_count)]
-            + [row_spec(queries.shape), row_spec(entries.shape), row_spec(marks.shape)],
-            out_specs=row_spec(queries.shape),
+            + [
+                whole(queries),
+                whole(entries),
+                pl.BlockSpec(
+                    (1,) + marks.shape[1:], lambda row, table_ref, length_ref: (row, 0, 0)
+                ),
+            ],
+            out_specs=whole(queries),
+            scratch_shapes=[
+                pltpu.VMEM((parts, queries.shape[0], head_dim), jnp.float32)
+                for parts in (heads, 2, heads)
+            ],
         ),
-        compiler_params=pltpu.CompilerParams(vmem_limit_bytes=40 * 2**20),
+        compiler_params=pltpu.CompilerParams(vmem_limit_bytes=48 * 2**20),
     )(local_table.reshape(-1), length, *([pool] * page_count), queries, entries, marks)
 
 
@@ -495,38 +563,27 @@
     )
     marks = jnp.concatenate(
         [
-            linked.astype(jnp.bfloat16),
-            held.reshape(rows, BEAMS * steps, 1).astype(jnp.bfloat16),
-            step_marks.reshape(rows, BEAMS * steps, 1).astype(jnp.bfloat16),
+            linked.astype(jnp.float32),
+            held.reshape(rows, BEAMS * steps, 1).astype(jnp.float32),
+            step_marks.reshape(rows, BEAMS * steps, 1).astype(jnp.float32),
         ],
         axis=2,
     )
-    mark_count = marks.shape[2]
-    marks = jnp.broadcast_to(
-        marks[:, :, None, :], (rows, BEAMS * steps, heads, mark_count)
-    ).reshape(rows, BEAMS * steps * heads, mark_count)
-
-    normed = rms_round(current, norm_attn)
+    current = gathered(current, kv_count, 1)
+    normed = rms_round(pick_half(current, halves, half).reshape(-1, width), norm_attn)
     query = jnp.dot(normed, w_query, preferred_element_type=jnp.float32).astype(jnp.bfloat16)
     fresh = jnp.dot(normed, w_keyval, preferred_element_type=jnp.float32).astype(jnp.bfloat16)
-    sent = jnp.concatenate([query, fresh], axis=1)
-    shared = pick_half(gathered(sent, kv_count, 1), halves, half)
-    shared = shared.reshape(BEAMS, steps, rows, -1).transpose(2, 0, 1, 3)
-    queries = shared[..., : heads * head_dim].reshape(rows, BEAMS * steps * heads, head_dim)
-    entries = shared[..., heads * head_dim :].reshape(rows, BEAMS * steps, 2 * head_dim)
-    answers = attend(
-        table - device * pool.shape[0], length, pool, queries, entries, marks
-    )
-    answers = answers.reshape(rows, BEAMS, steps, heads * head_dim).transpose(1, 2, 0, 3)
-    attended = reduced(
-        place_block(answers.reshape(BEAMS, steps * rows, heads * head_dim), halves, half), 2
+    answers = attend(table - device * pool.shape[0], length, pool, query, fresh, marks)
+    answers = answers.reshape(BEAMS, steps * rows, heads * head_dim)
+    attended = shared_sum(place_block(answers, halves, half), 2).reshape(-1, heads * head_dim)
+    residual = (
+        current.reshape(-1, width).astype(jnp.float32)
+        + jnp.dot(attended, w_out, preferred_element_type=jnp.float32)
     ).astype(jnp.bfloat16)
-    residual = (
-        current.astype(jnp.float32) + jnp.dot(attended, w_out, preferred_element_type=jnp.float32)
-    ).astype(jnp.bfloat16)
-    everyone = gathered(rms_round(residual, norm_mlp), kv_count, 3).reshape(-1, width)
-    terms = feed_forward(everyone, w_gate, w_up, w_down).astype(jnp.bfloat16)
-    summed = reduced(terms.reshape(kv_count, steps * rows, width), 4)
+    terms = feed_forward(rms_round(residual, norm_mlp), w_gate, w_up, w_down)
+    terms = terms.astype(jnp.bfloat16).reshape(kv_count, steps * rows, width)
+    summed = reduced(terms, 3)
+    residual = lax.dynamic_slice_in_dim(residual, member * steps * rows, steps * rows, 0)
     finished = (residual.astype(jnp.float32) + summed).astype(jnp.bfloat16)
     finished = finished.reshape(steps, rows, width)
     return reordered(by_target, swap(reordered(by_anchor.T, finished)))

time: 132 us -> 116 us (0.88)
  local copies, waits for them, and re-layouts: 18.1 us -> 4.7 us
  matrix products: 16.5 us -> 13.6 us
    pallas_call x3, Pallas kernels: 49.8 us -> 67.2 us  [the longest x1 33.6 us: shared_sum(): pl.pallas_call(functools.partial(share_kernel, count), out_shape=jax.Shap...]
    pallas_call x2 -> x1, Pallas kernels: 32.2 us -> 16 us  [reduced(): pl.pallas_call(functools.partial(reduce_kernel, count), out_shape=jax.Sha...]
    reshape x6 -> x0, local copies, waits for them, and re-layouts: 5.27 us -> none  [the longest x2 2.22 us: on_device(): answers.reshape(rows, BEAMS, steps, heads * head_dim).transpose(1, 2, 0, 3)]
    unnamed x34 -> x24, local copies, waits for them, and re-layouts: 3.28 us -> 0.08 us
    dot_general x1, matrix products: 3.48 us -> 1.49 us  [on_device(): jnp.dot(attended, w_out, preferred_element_type=jnp.float32)]
    slice x2 -> x0, local copies, waits for them, and re-layouts: 1.89 us -> none  [the longest x1 1.18 us: on_device(): shared[..., :heads * head_dim]]
    reshape x2, local copies, waits for them, and re-layouts: 1.59 us -> 0.08 us  [swap(): lax.all_to_all(shaped, 'req', split_axis=1, concat_axis=1, tiled=True)]
  transfers between devices with their start and end apart: 1 -> 1, of which waited for: 0 -> 1; matrix products, arithmetic and copies ran while one was open for 3% -> 3% of each run, Pallas kernels for 0% -> 0%
where the time goes in v3:
time: 116 us; the launch traced here: 115 us
  Pallas kernels  83.2 us (72%)
  matrix products  13.6 us (12%)
  blocking collectives  6.96 us (6%)
  local copies, waits for them, and re-layouts  4.7 us (4%)
  starting transfers between devices  4.21 us (4%)
  other arithmetic  2.03 us (2%)
    pallas_call x1, Pallas kernels, shared_sum(): pl.pallas_call(functools.partial(share_kernel, count), out_shape=jax.Shap...  33.6 us
    pallas_call x1, Pallas kernels, gathered(): pl.pallas_call(functools.partial(gather_kernel, count, True), out_shape=j...  19.5 us
    pallas_call x1, Pallas kernels, reduced(): pl.pallas_call(functools.partial(reduce_kernel, count), out_shape=jax.Sha...  16 us
    pallas_call x1, Pallas kernels, attend(): pl.pallas_call(functools.partial(attention_kernel, page_count, heads, row...  14.2 us
    all_to_all x1, blocking collectives, swap(): lax.all_to_all(shaped, 'req', split_axis=1, concat_axis=1, tiled=True)  6.96 us
    all_to_all x1, starting transfers between devices, swap(): lax.all_to_all(shaped, 'req', split_axis=1, concat_axis=1, tiled=True)  4.21 us
    dot_general x1, matrix products, feed_forward(): return jnp.dot(hidden, w_down, preferred_element_type=jnp.float32)  3.94 us
    dot_general x1, matrix products, on_device(): jnp.dot(normed, w_query, preferred_element_type=jnp.float32)  3.87 us
  transfers between devices with their start and end apart: 1, of which 1 were waited for; matrix products, arithmetic and copies ran while one was open for 3% of the time, Pallas kernels for 0%

profile of v3, /device:TPU:0, one launch (start us, length us, event | category | flops | bytes accessed | tf_op | source)
XLA Modules:
  0.0 115.3 jit_solution(666265102221176169)
XLA Ops:
  0.0 0.9 reshape.192
  1.1 1.2 %fusion.1 = bf16[4,8,1536]{2,1,0:T(8,128)(2,1)S(1)} fusion(bf16[4,8,1536]{2,1,0:T(8,128)(2,1)} %param.14, s32[8]{0:T(128)S(1)} %multiply_add_fusion.1), kind=kOutput, calls=%fused_computation.9 | convolution fusion | flops 835648 | bytes 196640 | tf_op jit(solution)/shard_map/pi,tiw->tpw/dot_general | solution.py:384
  2.3 0.7 copy.38
  3.0 4.2 %all-to-all-start = ((bf16[4,4,2,1536]{3,2,0,1:T(2,128)(2,1)}), bf16[4,4,2,1536]{3,2,0,1:T(2,128)(2,1)S(1)}, u32[]{:S(2)}, u32[]{:S(2)}) async-start(bf16[4,4,2,1536]{3,2,0,1:T(2,128)(2,1)} %copy.38), calls=%async_computation | async-start | bytes 196608 | tf_op jit(solution)/shard_map/all_to_all | solution.py:534
  7.6 0.7 broadcast_subtract_fusion
  8.5 0.8 constant_dynamic-slice_fusion
  9.8 0.3 copy.44
  10.1 0.3 copy.45
  10.4 0.2 copy.42
  10.6 0.6 gather_fusion
  11.7 0.2 fusion.2.own_ref
  11.9 19.5 %shard_map.136 = bf16[8,32,1536]{2,1,0:T(8,128)(2,1)S(1)} custom-call(bf16[32,1536]{1,0:T(8,128)(2,1)S(1)} %fusion.2.own_ref), custom_call_target="tpu_custom_call" | custom-call | tf_op jit(solution)/shard_map/pallas_call | solution.py:163
  31.4 0.2 multiply_reduce_fusion
  31.7 0.3 fusion.9
  32.0 0.4 convolution_convert_fusion.6.refs_10_
  32.4 3.9 %convolution_convert_fusion.1.refs_9_ = bf16[256,1536]{1,0:T(8,128)(2,1)S(1)} fusion(bf16[256,1536]{1,0:T(8,128)(2,1)S(1)} %fusion.9, bf16[1536,1536]{1,0:T(8,128)(2,1)} %param.21), kind=kOutput, calls=%fused_computation.4 | convolution fusion | flops 1208352768 | bytes 6291456 | tf_op jit(solution)/shard_map/dot_general | solution.py:574
  36.3 14.2 %shard_map.137 = bf16[256,1536]{1,0:T(8,128)(2,1)S(1)} custom-call(s32[72]{0:T(128)S(1)} %reshape.196.table_ref, s32[8]{0:T(128)S(1)} %gather_fusion, bf16[72,128,256]{2,1,0:T(8,128)(2,1)} %refs_8_.1, bf16[72,128,256]{2,1,0:T(8,128)(2,1)} %refs_8_.1, bf16[72,128,256]{2,1,0:T(8,128)(2,1)} %refs_8_.1, bf16[72,128,256]{2,1,0:T(8,128)(2,1)} %refs_8_.1, ...), custom_call_target="tpu_custom_call" | custom-call | tf_op jit(solution)/shard_map/pallas_call | solution.py:465
  50.5 33.6 %shard_map.138 = bf16[8,32,1536]{2,1,0:T(8,128)(2,1)S(1)} custom-call(bf16[8,32,1536]{2,1,0:T(8,128)(2,1)S(1)} %bitcast.103), custom_call_target="tpu_custom_call" | custom-call | tf_op jit(solution)/shard_map/pallas_call | solution.py:366
  84.1 1.5 %fusion.5 = (f32[256]{0:T(256)S(1)}, bf16[256,1536]{1,0:T(8,128)(2,1)S(1)}) fusion(bf16[256,1536]{1,0:T(8,128)(2,1)S(1)} %bitcast.104, bf16[1536,1536]{1,0:T(8,128)(2,1)S(1)} %bitcast.118, bf16[256,1536]{1,0:T(8,128)(2,1)S(1)} %bitcast.102), kind=kOutput, calls=%fused_computation.15 | convolution fusion | flops 1210318592 | bytes 7078912 | tf_op jit(solution)/shard_map/dot_general | solution.py:581
  85.6 1.6 %fusion.25 = f32[256,576]{0,1:T(8,128)} fusion(bf16[1536,576]{0,1:T(8,128)(2,1)S(1)} %copy-done.4, bf16[256,1536]{1,0:T(8,128)(2,1)S(1)} %get-tuple-element.21, f32[1536]{0:T(1024)S(1)} %copy-done.5, f32[256]{0:T(256)S(1)} %add_rsqrt_fusion.1), kind=kOutput, calls=%fused_computation.37 | convolution fusion | flops 454557696 | bytes 3152896 | tf_op jit(solution)/shard_map/dot_general | solution.py:26
  87.2 3.9 %convolution_convert_fusion = bf16[256,1536]{1,0:T(8,128)(2,1)S(1)} fusion(bf16[576,1536]{1,0:T(8,128)(2,1)S(1)} %copy-done, bf16[1536,576]{0,1:T(8,128)(2,1)} %param.26, f32[256,576]{0,1:T(8,128)} %fusion.25, bf16[256,1536]{1,0:T(8,128)(2,1)S(1)} %get-tuple-element.21, f32[1536]{0:T(1024)S(1)} %copy-done.5, f32[256]{0:T(256)S(1)} %add_rsqrt_fusion.1), kind=kOutput, calls=%fused_computation.3 | convolution fusion | flops 909410304 | bytes 5708800 | tf_op jit(solution)/shard_map/dot_general | solution.py:29
  91.1 16.0 %shard_map.139 = f32[32,1536]{1,0:T(8,128)S(1)} custom-call(bf16[8,32,1536]{2,1,0:T(8,128)(2,1)S(1)} %bitcast.105), custom_call_target="tpu_custom_call" | custom-call | tf_op jit(solution)/shard_map/pallas_call | solution.py:345
  107.4 7.0 %all_to_all.10 = bf16[4,4,2,1536]{3,2,0,1:T(2,128)(2,1)S(1)} all-to-all(bf16[4,4,2,1536]{3,2,0,1:T(2,128)(2,1)S(1)} %copy.46), channel_id=1, replica_groups=mesh['req'=4,'kv'=8] {'req'}, dimensions={1} | all-to-all | bytes 196608 | tf_op jit(solution)/shard_map/all_to_all | solution.py:534
  114.5 0.9 fusion.4
  (73 shorter events, 2.1 us)
Async XLA Ops:
  0.0 87.2 %copy-start = (bf16[576,1536]{1,0:T(8,128)(2,1)S(1)}, bf16[576,1536]{1,0:T(8,128)(2,1)}, u32[]{:S(2)}) copy-start(bf16[576,1536]{1,0:T(8,128)(2,1)} %param.27) | copy-start | bytes 5308420
  2.3 8.4 %copy-start.1 = (s32[32]{0:T(128)S(1)}, s32[32]{0:T(128)}, u32[]{:S(2)}) copy-start(s32[32]{0:T(128)} %param.15) | copy-start | bytes 388
  3.0 8.5 %all-to-all-start = ((bf16[4,4,2,1536]{3,2,0,1:T(2,128)(2,1)}), bf16[4,4,2,1536]{3,2,0,1:T(2,128)(2,1)S(1)}, u32[]{:S(2)}, u32[]{:S(2)}) async-start(bf16[4,4,2,1536]{3,2,0,1:T(2,128)(2,1)} %copy.38), calls=%async_computation | async-start | bytes 196608 | tf_op jit(solution)/shard_map/all_to_all | solution.py:534
  11.3 20.4 %copy-start.3 = (f32[1536]{0:T(1024)S(1)}, f32[1536]{0:T(1024)}, u32[]{:S(2)}) copy-start(f32[1536]{0:T(1024)} %param.20) | copy-start | bytes 18436
  11.9 20.1 %copy-start.2 = (bf16[1536,256]{1,0:T(8,128)(2,1)S(1)}, bf16[1536,256]{1,0:T(8,128)(2,1)}, u32[]{:S(2)}) copy-start(bf16[1536,256]{1,0:T(8,128)(2,1)} %param.22) | copy-start | bytes 2359300
  32.4 51.7 %slice-start = ((s8[4718592]{0:T(1024)(128)(4,1)}), s8[4194304]{0:T(1024)(128)(4,1)S(1)}, s32[]{:S(2)}) async-start(s8[4718592]{0:T(1024)(128)(4,1)} %bitcast.117), calls=%async_computation.2 | async-start | bytes 8388608
  36.3 47.8 %slice-start.1 = ((s8[4718592]{0:T(1024)(128)(4,1)}), s8[524288]{0:T(1024)(128)(4,1)S(1)}, s32[]{:S(2)}) async-start(s8[4718592]{0:T(1024)(128)(4,1)} %bitcast.117), calls=%async_computation.3 | async-start | bytes 1048576
  84.1 1.5 %copy-start.4 = (bf16[1536,576]{0,1:T(8,128)(2,1)S(1)}, bf16[1536,576]{0,1:T(8,128)(2,1)}, u32[]{:S(2)}) copy-start(bf16[1536,576]{0,1:T(8,128)(2,1)} %param.25) | copy-start | bytes 5308420
  84.1 1.5 %copy-start.5 = (f32[1536]{0:T(1024)S(1)}, f32[1536]{0:T(1024)}, u32[]{:S(2)}) copy-start(f32[1536]{0:T(1024)} %param.24) | copy-start | bytes 18436

commit v4 on v3

--- a/solution.py
+++ b/solution.py
@@ -117,26 +117,35 @@
     pl.semaphore_wait(barrier, 1 + above.astype(jnp.int32) + below.astype(jnp.int32))
 
 
+def column_widths(count, width):
+    short = max(width // (count - 2) // 128 * 128, 128)
+    return width - short, short
+
+
+def column_parts(count, width):
+    long, short = column_widths(count, width)
+    return pl.ds(0, long), pl.ds(long, short)
+
+
 def gather_kernel(count, greeting, own_ref, all_ref, send_sem, first_sem, second_sem):
     me, low, high, length, above, below, partner, up, down = place_on_lines(count)
-    middle = own_ref.shape[0] // 2
-    first, second = pl.ds(0, middle), pl.ds(middle, middle)
+    first, second = column_parts(count, own_ref.shape[1])
     if greeting:
         greet(above, below, partner, up, down)
     sends = Sends(send_sem)
 
     def spread(where, block, source, part, sems, peer):
-        sends.go(where, source, all_ref.at[block, part], sems.at[block], peer)
-
-    spread(None, me, own_ref.at[second], second, second_sem, partner)
+        sends.go(where, source, all_ref.at[block, :, part], sems.at[block], peer)
+
+    spread(None, me, own_ref.at[:, second], second, second_sem, partner)
     for where, peer in ((above, up), (below, down)):
-        spread(where, me, own_ref.at[first], first, first_sem, peer)
-        spread(where, me, own_ref.at[second], second, second_sem, peer)
-    spread(None, me, own_ref.at[first], first, first_sem, partner)
+        spread(where, me, own_ref.at[:, first], first, first_sem, peer)
+        spread(where, me, own_ref.at[:, second], second, second_sem, peer)
+    spread(None, me, own_ref.at[:, first], first, first_sem, partner)
     all_ref[me] = own_ref[...]
-    landed(None, all_ref.at[partner, second], second_sem.at[partner])
+    landed(None, all_ref.at[partner, :, second], second_sem.at[partner])
     for where, peer in ((above, up), (below, down)):
-        spread(where, partner, all_ref.at[partner, second], second, second_sem, peer)
+        spread(where, partner, all_ref.at[partner, :, second], second, second_sem, peer)
     for distance in range(1, length):
         for source, here, where, peer in (
             (jnp.maximum(high - distance, 0), high >= distance, above, up),
@@ -145,16 +154,16 @@
             same = source * 2 + low
             cross = source * 2 + 1 - low
             onward = here & where
-            landed(here, all_ref.at[same, first], first_sem.at[same])
-            spread(onward, same, all_ref.at[same, first], first, first_sem, peer)
-            spread(here, same, all_ref.at[same, first], first, first_sem, partner)
-            landed(here, all_ref.at[same, second], second_sem.at[same])
-            spread(onward, same, all_ref.at[same, second], second, second_sem, peer)
-            landed(here, all_ref.at[cross, second], second_sem.at[cross])
-            spread(onward, cross, all_ref.at[cross, second], second, second_sem, peer)
+            landed(here, all_ref.at[same, :, first], first_sem.at[same])
+            spread(onward, same, all_ref.at[same, :, first], first, first_sem, peer)
+            spread(here, same, all_ref.at[same, :, first], first, first_sem, partner)
+            landed(here, all_ref.at[same, :, second], second_sem.at[same])
+            spread(onward, same, all_ref.at[same, :, second], second, second_sem, peer)
+            landed(here, all_ref.at[cross, :, second], second_sem.at[cross])
+            spread(onward, cross, all_ref.at[cross, :, second], second, second_sem, peer)
     for line in range(length):
         cross = line * 2 + 1 - low
-        landed(None, all_ref.at[cross, first], first_sem.at[cross])
+        landed(None, all_ref.at[cross, :, first], first_sem.at[cross])
     sends.finish()
 
 
@@ -191,14 +200,13 @@
     down_sem,
 ):
     me, low, high, length, above, below, partner, up, down = place_on_lines(count)
-    middle = sum_ref.shape[0] // 2
-    first, second = pl.ds(0, middle), pl.ds(middle, middle)
+    first, second = column_parts(count, sum_ref.shape[1])
     greet(above, below, partner, up, down)
     sends = Sends(send_sem)
     for line in range(length):
         sends.go(
             None,
-            terms_ref.at[line * 2 + 1 - low, first],
+            terms_ref.at[line * 2 + 1 - low, :, first],
             cross_first.at[line],
             cross_sem.at[line],
             partner,
@@ -208,7 +216,7 @@
         return ref[...].astype(jnp.float32)
 
     def base_first(line):
-        return wide(terms_ref.at[line * 2 + low, first]) + wide(cross_first.at[line])
+        return wide(terms_ref.at[line * 2 + low, :, first]) + wide(cross_first.at[line])
 
     def pass_on(here, line, behind, slot, stage, arrived, ahead, base):
         def with_slot():
@@ -242,7 +250,7 @@
                     stage_second.at[block],
                     sems.at[length + block],
                     ahead,
-                    lambda block=block: wide(terms_ref.at[block, second]),
+                    lambda block=block: wide(terms_ref.at[block, :, second]),
                 )
     for line in range(length):
         landed(None, cross_first.at[line], cross_sem.at[line])
@@ -263,12 +271,12 @@
             )
 
     def collect(into, part, value, up_slot, down_slot, up_arrived, down_arrived):
-        into[part, :] = value
+        into[:, part] = value
         landed(below, up_slot, up_arrived)
         landed(above, down_slot, down_arrived)
 
         def add(slot):
-            into[part, :] += wide(slot)
+            into[:, part] += wide(slot)
 
         pl.when(below)(lambda: add(up_slot))
         pl.when(above)(lambda: add(down_slot))
@@ -276,18 +284,18 @@
     collect(
         sum_ref,
         second,
-        wide(terms_ref.at[partner, second]),
+        wide(terms_ref.at[partner, :, second]),
         up_second.at[partner],
         down_second.at[partner],
         up_sem.at[length + partner],
         down_sem.at[length + partner],
     )
-    stage_cross[...] = sum_ref[second, :].astype(stage_cross.dtype)
+    stage_cross[...] = sum_ref[:, second].astype(stage_cross.dtype)
     sends.go(None, stage_cross, cross_second, cross_sem.at[length], partner)
     collect(
         sum_ref,
         second,
-        wide(terms_ref.at[me, second]),
+        wide(terms_ref.at[me, :, second]),
         up_second.at[me],
         down_second.at[me],
         up_sem.at[length + me],
@@ -303,7 +311,7 @@
         down_sem.at[high],
     )
     landed(None, cross_second, cross_sem.at[length])
-    sum_ref[second, :] += wide(cross_second)
+    sum_ref[:, second] += wide(cross_second)
     sends.finish()
 
 
@@ -319,19 +327,21 @@
     count, rows, width = terms.shape
     length = count // 2
 
-    def slots(*shape):
-        return pltpu.VMEM(shape + (rows // 2, width), terms.dtype)
+    long, short = column_widths(count, width)
+
+    def slots(columns, *shape):
+        return pltpu.VMEM(shape + (rows, columns), terms.dtype)
 
     return [
-        slots(length),
-        slots(length),
-        slots(length),
-        slots(length),
-        slots(),
-        slots(count),
-        slots(count),
-        slots(count),
-        slots(),
+        slots(long, length),
+        slots(long, length),
+        slots(long, length),
+        slots(long, length),
+        slots(short),
+        slots(short, count),
+        slots(short, count),
+        slots(short, count),
+        slots(short),
         pltpu.SemaphoreType.DMA((8 * length,)),
         pltpu.SemaphoreType.DMA((length + 1,)),
         pltpu.SemaphoreType.DMA((length + count,)),

time: 116 us -> 119 us (1.026); the launches traced: 115 us -> 117 us
  Pallas kernels: 83.2 us -> 85.1 us
    pallas_call x1, Pallas kernels: 33.6 us -> 35.6 us  [shared_sum(): pl.pallas_call(functools.partial(share_kernel, count), out_shape=jax.Shap...]
where the time goes in v4:
time: 119 us; the launch traced here: 117 us
  Pallas kernels  85.1 us (72%)
  matrix products  13.6 us (11%)
  blocking collectives  6.79 us (6%)
  local copies, waits for them, and re-layouts  4.7 us (4%)
  starting transfers between devices  4.21 us (4%)
  other arithmetic  2.03 us (2%)
    pallas_call x1, Pallas kernels, shared_sum(): pl.pallas_call(functools.partial(share_kernel, count), out_shape=jax.Shap...  35.6 us
    pallas_call x1, Pallas kernels, gathered(): pl.pallas_call(functools.partial(gather_kernel, count, True), out_shape=j...  19.3 us
    pallas_call x1, Pallas kernels, reduced(): pl.pallas_call(functools.partial(reduce_kernel, count), out_shape=jax.Sha...  16 us
    pallas_call x1, Pallas kernels, attend(): pl.pallas_call(functools.partial(attention_kernel, page_count, heads, row...  14.2 us
    all_to_all x1, blocking collectives, swap(): lax.all_to_all(shaped, 'req', split_axis=1, concat_axis=1, tiled=True)  6.79 us
    all_to_all x1, starting transfers between devices, swap(): lax.all_to_all(shaped, 'req', split_axis=1, concat_axis=1, tiled=True)  4.21 us
    dot_general x1, matrix products, feed_forward(): return jnp.dot(hidden, w_down, preferred_element_type=jnp.float32)  3.94 us
    dot_general x1, matrix products, on_device(): jnp.dot(normed, w_query, preferred_element_type=jnp.float32)  3.87 us
  transfers between devices with their start and end apart: 1, of which 1 were waited for; matrix products, arithmetic and copies ran while one was open for 3% of the time, Pallas kernels for 0%

profile of v4, /device:TPU:0, one launch (start us, length us, event | category | flops | bytes accessed | tf_op | source)
XLA Modules:
  0.0 117.0 jit_solution(1488021183720272052)
XLA Ops:
  0.0 0.9 reshape.192
  1.1 1.2 %fusion.1 = bf16[4,8,1536]{2,1,0:T(8,128)(2,1)S(1)} fusion(bf16[4,8,1536]{2,1,0:T(8,128)(2,1)} %param.14, s32[8]{0:T(128)S(1)} %multiply_add_fusion.1), kind=kOutput, calls=%fused_computation.9 | convolution fusion | flops 835648 | bytes 196640 | tf_op jit(solution)/shard_map/pi,tiw->tpw/dot_general | solution.py:394
  2.3 0.7 copy.38
  3.0 4.2 %all-to-all-start = ((bf16[4,4,2,1536]{3,2,0,1:T(2,128)(2,1)}), bf16[4,4,2,1536]{3,2,0,1:T(2,128)(2,1)S(1)}, u32[]{:S(2)}, u32[]{:S(2)}) async-start(bf16[4,4,2,1536]{3,2,0,1:T(2,128)(2,1)} %copy.38), calls=%async_computation | async-start | bytes 196608 | tf_op jit(solution)/shard_map/all_to_all | solution.py:544
  7.6 0.7 broadcast_subtract_fusion
  8.5 0.8 constant_dynamic-slice_fusion
  9.8 0.3 copy.44
  10.1 0.3 copy.45
  10.4 0.2 copy.42
  10.6 0.6 gather_fusion
  11.7 0.2 fusion.2.own_ref
  11.9 19.3 %shard_map.136 = bf16[8,32,1536]{2,1,0:T(8,128)(2,1)S(1)} custom-call(bf16[32,1536]{1,0:T(8,128)(2,1)S(1)} %fusion.2.own_ref), custom_call_target="tpu_custom_call" | custom-call | tf_op jit(solution)/shard_map/pallas_call | solution.py:172
  31.2 0.2 multiply_reduce_fusion
  31.5 0.3 fusion.9
  31.8 0.4 convolution_convert_fusion.6.refs_10_
  32.2 3.9 %convolution_convert_fusion.1.refs_9_ = bf16[256,1536]{1,0:T(8,128)(2,1)S(1)} fusion(bf16[256,1536]{1,0:T(8,128)(2,1)S(1)} %fusion.9, bf16[1536,1536]{1,0:T(8,128)(2,1)} %param.21), kind=kOutput, calls=%fused_computation.4 | convolution fusion | flops 1208352768 | bytes 6291456 | tf_op jit(solution)/shard_map/dot_general | solution.py:584
  36.1 14.2 %shard_map.137 = bf16[256,1536]{1,0:T(8,128)(2,1)S(1)} custom-call(s32[72]{0:T(128)S(1)} %reshape.196.table_ref, s32[8]{0:T(128)S(1)} %gather_fusion, bf16[72,128,256]{2,1,0:T(8,128)(2,1)} %refs_8_.1, bf16[72,128,256]{2,1,0:T(8,128)(2,1)} %refs_8_.1, bf16[72,128,256]{2,1,0:T(8,128)(2,1)} %refs_8_.1, bf16[72,128,256]{2,1,0:T(8,128)(2,1)} %refs_8_.1, ...), custom_call_target="tpu_custom_call" | custom-call | tf_op jit(solution)/shard_map/pallas_call | solution.py:475
  50.3 35.6 %shard_map.138 = bf16[8,32,1536]{2,1,0:T(8,128)(2,1)S(1)} custom-call(bf16[8,32,1536]{2,1,0:T(8,128)(2,1)S(1)} %bitcast.103), custom_call_target="tpu_custom_call" | custom-call | tf_op jit(solution)/shard_map/pallas_call | solution.py:376
  86.0 1.5 %fusion.5 = (f32[256]{0:T(256)S(1)}, bf16[256,1536]{1,0:T(8,128)(2,1)S(1)}) fusion(bf16[256,1536]{1,0:T(8,128)(2,1)S(1)} %bitcast.104, bf16[1536,1536]{1,0:T(8,128)(2,1)S(1)} %bitcast.118, bf16[256,1536]{1,0:T(8,128)(2,1)S(1)} %bitcast.102), kind=kOutput, calls=%fused_computation.15 | convolution fusion | flops 1210318592 | bytes 7078912 | tf_op jit(solution)/shard_map/dot_general | solution.py:591
  87.5 1.6 %fusion.25 = f32[256,576]{0,1:T(8,128)} fusion(bf16[1536,576]{0,1:T(8,128)(2,1)S(1)} %copy-done.4, bf16[256,1536]{1,0:T(8,128)(2,1)S(1)} %get-tuple-element.21, f32[1536]{0:T(1024)S(1)} %copy-done.5, f32[256]{0:T(256)S(1)} %add_rsqrt_fusion.1), kind=kOutput, calls=%fused_computation.37 | convolution fusion | flops 454557696 | bytes 3152896 | tf_op jit(solution)/shard_map/dot_general | solution.py:26
  89.0 3.9 %convolution_convert_fusion = bf16[256,1536]{1,0:T(8,128)(2,1)S(1)} fusion(bf16[576,1536]{1,0:T(8,128)(2,1)S(1)} %copy-done, bf16[1536,576]{0,1:T(8,128)(2,1)} %param.26, f32[256,576]{0,1:T(8,128)} %fusion.25, bf16[256,1536]{1,0:T(8,128)(2,1)S(1)} %get-tuple-element.21, f32[1536]{0:T(1024)S(1)} %copy-done.5, f32[256]{0:T(256)S(1)} %add_rsqrt_fusion.1), kind=kOutput, calls=%fused_computation.3 | convolution fusion | flops 909410304 | bytes 5708800 | tf_op jit(solution)/shard_map/dot_general | solution.py:29
  93.0 16.0 %shard_map.139 = f32[32,1536]{1,0:T(8,128)S(1)} custom-call(bf16[8,32,1536]{2,1,0:T(8,128)(2,1)S(1)} %bitcast.105), custom_call_target="tpu_custom_call" | custom-call | tf_op jit(solution)/shard_map/pallas_call | solution.py:355
  109.2 6.8 %all_to_all.10 = bf16[4,4,2,1536]{3,2,0,1:T(2,128)(2,1)S(1)} all-to-all(bf16[4,4,2,1536]{3,2,0,1:T(2,128)(2,1)S(1)} %copy.46), channel_id=1, replica_groups=mesh['req'=4,'kv'=8] {'req'}, dimensions={1} | all-to-all | bytes 196608 | tf_op jit(solution)/shard_map/all_to_all | solution.py:544
  116.2 0.9 fusion.4
  (73 shorter events, 2.1 us)
Async XLA Ops:
  0.0 89.0 %copy-start = (bf16[576,1536]{1,0:T(8,128)(2,1)S(1)}, bf16[576,1536]{1,0:T(8,128)(2,1)}, u32[]{:S(2)}) copy-start(bf16[576,1536]{1,0:T(8,128)(2,1)} %param.27) | copy-start | bytes 5308420
  2.3 8.4 %copy-start.1 = (s32[32]{0:T(128)S(1)}, s32[32]{0:T(128)}, u32[]{:S(2)}) copy-start(s32[32]{0:T(128)} %param.15) | copy-start | bytes 388
  3.0 8.5 %all-to-all-start = ((bf16[4,4,2,1536]{3,2,0,1:T(2,128)(2,1)}), bf16[4,4,2,1536]{3,2,0,1:T(2,128)(2,1)S(1)}, u32[]{:S(2)}, u32[]{:S(2)}) async-start(bf16[4,4,2,1536]{3,2,0,1:T(2,128)(2,1)} %copy.38), calls=%async_computation | async-start | bytes 196608 | tf_op jit(solution)/shard_map/all_to_all | solution.py:544
  11.3 20.2 %copy-start.3 = (f32[1536]{0:T(1024)S(1)}, f32[1536]{0:T(1024)}, u32[]{:S(2)}) copy-start(f32[1536]{0:T(1024)} %param.20) | copy-start | bytes 18436
  11.9 19.9 %copy-start.2 = (bf16[1536,256]{1,0:T(8,128)(2,1)S(1)}, bf16[1536,256]{1,0:T(8,128)(2,1)}, u32[]{:S(2)}) copy-start(bf16[1536,256]{1,0:T(8,128)(2,1)} %param.22) | copy-start | bytes 2359300
  32.2 53.7 %slice-start = ((s8[4718592]{0:T(1024)(128)(4,1)}), s8[4194304]{0:T(1024)(128)(4,1)S(1)}, s32[]{:S(2)}) async-start(s8[4718592]{0:T(1024)(128)(4,1)} %bitcast.117), calls=%async_computation.2 | async-start | bytes 8388608
  36.1 49.8 %slice-start.1 = ((s8[4718592]{0:T(1024)(128)(4,1)}), s8[524288]{0:T(1024)(128)(4,1)S(1)}, s32[]{:S(2)}) async-start(s8[4718592]{0:T(1024)(128)(4,1)} %bitcast.117), calls=%async_computation.3 | async-start | bytes 1048576
  85.9 1.5 %copy-start.4 = (bf16[1536,576]{0,1:T(8,128)(2,1)S(1)}, bf16[1536,576]{0,1:T(8,128)(2,1)}, u32[]{:S(2)}) copy-start(bf16[1536,576]{0,1:T(8,128)(2,1)} %param.25) | copy-start | bytes 5308420
  85.9 1.5 %copy-start.5 = (f32[1536]{0:T(1024)S(1)}, f32[1536]{0:T(1024)}, u32[]{:S(2)}) copy-start(f32[1536]{0:T(1024)} %param.24) | copy-start | bytes 18436

commit v5 on v3

--- a/solution.py
+++ b/solution.py
@@ -244,13 +244,11 @@
                     ahead,
                     lambda block=block: wide(terms_ref.at[block, second]),
                 )
-    for line in range(length):
-        landed(None, cross_first.at[line], cross_sem.at[line])
-    for distance in range(length - 1, 0, -1):
         for sign, behind, _, slot, sems, ahead in directions:
             line = high + sign * distance
             here = (line < length) & (line >= 0)
             line = jnp.clip(line, 0, length - 1)
+            landed(here, cross_first.at[line], cross_sem.at[line])
             pass_on(
                 here,
                 line,
@@ -261,6 +259,7 @@
                 ahead,
                 lambda line=line: base_first(line),
             )
+    landed(None, cross_first.at[high], cross_sem.at[high])
 
     def collect(into, part, value, up_slot, down_slot, up_arrived, down_arrived):
         into[part, :] = value

time: 116 us -> 117 us (level)
  Pallas kernels: 83.2 us -> 84.5 us
    pallas_call x1, Pallas kernels: 16 us -> 17.8 us  [reduced(): pl.pallas_call(functools.partial(reduce_kernel, count), out_shape=jax.Sha...]
where the time goes in v5:
time: 117 us
  Pallas kernels  84.5 us (72%)
  matrix products  13.6 us (12%)
  blocking collectives  6.98 us (6%)
  local copies, waits for them, and re-layouts  4.7 us (4%)
  starting transfers between devices  4.21 us (4%)
  other arithmetic  2.03 us (2%)
    pallas_call x1, Pallas kernels, shared_sum(): pl.pallas_call(functools.partial(share_kernel, count), out_shape=jax.Shap...  33 us
    pallas_call x1, Pallas kernels, gathered(): pl.pallas_call(functools.partial(gather_kernel, count, True), out_shape=j...  19.5 us
    pallas_call x1, Pallas kernels, reduced(): pl.pallas_call(functools.partial(reduce_kernel, count), out_shape=jax.Sha...  17.8 us
    pallas_call x1, Pallas kernels, attend(): pl.pallas_call(functools.partial(attention_kernel, page_count, heads, row...  14.2 us
    all_to_all x1, blocking collectives, swap(): lax.all_to_all(shaped, 'req', split_axis=1, concat_axis=1, tiled=True)  6.98 us
    all_to_all x1, starting transfers between devices, swap(): lax.all_to_all(shaped, 'req', split_axis=1, concat_axis=1, tiled=True)  4.21 us
    dot_general x1, matrix products, feed_forward(): return jnp.dot(hidden, w_down, preferred_element_type=jnp.float32)  3.94 us
    dot_general x1, matrix products, on_device(): jnp.dot(normed, w_query, preferred_element_type=jnp.float32)  3.87 us
  transfers between devices with their start and end apart: 1, of which 1 were waited for; matrix products, arithmetic and copies ran while one was open for 3% of the time, Pallas kernels for 0%

profile of v5, /device:TPU:0, one launch (start us, length us, event | category | flops | bytes accessed | tf_op | source)
XLA Modules:
  0.0 116.6 jit_solution(2790165452482590284)
XLA Ops:
  0.0 0.9 reshape.192
  1.1 1.2 %fusion.1 = bf16[4,8,1536]{2,1,0:T(8,128)(2,1)S(1)} fusion(bf16[4,8,1536]{2,1,0:T(8,128)(2,1)} %param.14, s32[8]{0:T(128)S(1)} %multiply_add_fusion.1), kind=kOutput, calls=%fused_computation.9 | convolution fusion | flops 835648 | bytes 196640 | tf_op jit(solution)/shard_map/pi,tiw->tpw/dot_general | solution.py:383
  2.3 0.7 copy.38
  3.0 4.2 %all-to-all-start = ((bf16[4,4,2,1536]{3,2,0,1:T(2,128)(2,1)}), bf16[4,4,2,1536]{3,2,0,1:T(2,128)(2,1)S(1)}, u32[]{:S(2)}, u32[]{:S(2)}) async-start(bf16[4,4,2,1536]{3,2,0,1:T(2,128)(2,1)} %copy.38), calls=%async_computation | async-start | bytes 196608 | tf_op jit(solution)/shard_map/all_to_all | solution.py:533
  7.6 0.7 broadcast_subtract_fusion
  8.5 0.8 constant_dynamic-slice_fusion
  9.8 0.3 copy.44
  10.1 0.3 copy.45
  10.4 0.2 copy.42
  10.6 0.6 gather_fusion
  11.7 0.2 fusion.2.own_ref
  11.9 19.5 %shard_map.136 = bf16[8,32,1536]{2,1,0:T(8,128)(2,1)S(1)} custom-call(bf16[32,1536]{1,0:T(8,128)(2,1)S(1)} %fusion.2.own_ref), custom_call_target="tpu_custom_call" | custom-call | tf_op jit(solution)/shard_map/pallas_call | solution.py:163
  31.4 0.2 multiply_reduce_fusion
  31.7 0.3 fusion.9
  32.0 0.4 convolution_convert_fusion.6.refs_10_
  32.4 3.9 %convolution_convert_fusion.1.refs_9_ = bf16[256,1536]{1,0:T(8,128)(2,1)S(1)} fusion(bf16[256,1536]{1,0:T(8,128)(2,1)S(1)} %fusion.9, bf16[1536,1536]{1,0:T(8,128)(2,1)} %param.21), kind=kOutput, calls=%fused_computation.4 | convolution fusion | flops 1208352768 | bytes 6291456 | tf_op jit(solution)/shard_map/dot_general | solution.py:573
  36.3 14.2 %shard_map.137 = bf16[256,1536]{1,0:T(8,128)(2,1)S(1)} custom-call(s32[72]{0:T(128)S(1)} %reshape.196.table_ref, s32[8]{0:T(128)S(1)} %gather_fusion, bf16[72,128,256]{2,1,0:T(8,128)(2,1)} %refs_8_.1, bf16[72,128,256]{2,1,0:T(8,128)(2,1)} %refs_8_.1, bf16[72,128,256]{2,1,0:T(8,128)(2,1)} %refs_8_.1, bf16[72,128,256]{2,1,0:T(8,128)(2,1)} %refs_8_.1, ...), custom_call_target="tpu_custom_call" | custom-call | tf_op jit(solution)/shard_map/pallas_call | solution.py:464
  50.5 33.0 %shard_map.138 = bf16[8,32,1536]{2,1,0:T(8,128)(2,1)S(1)} custom-call(bf16[8,32,1536]{2,1,0:T(8,128)(2,1)S(1)} %bitcast.103), custom_call_target="tpu_custom_call" | custom-call | tf_op jit(solution)/shard_map/pallas_call | solution.py:365
  83.5 1.5 %fusion.5 = (f32[256]{0:T(256)S(1)}, bf16[256,1536]{1,0:T(8,128)(2,1)S(1)}) fusion(bf16[256,1536]{1,0:T(8,128)(2,1)S(1)} %bitcast.104, bf16[1536,1536]{1,0:T(8,128)(2,1)S(1)} %bitcast.118, bf16[256,1536]{1,0:T(8,128)(2,1)S(1)} %bitcast.102), kind=kOutput, calls=%fused_computation.15 | convolution fusion | flops 1210318592 | bytes 7078912 | tf_op jit(solution)/shard_map/dot_general | solution.py:580
  85.1 1.6 %fusion.25 = f32[256,576]{0,1:T(8,128)} fusion(bf16[1536,576]{0,1:T(8,128)(2,1)S(1)} %copy-done.4, bf16[256,1536]{1,0:T(8,128)(2,1)S(1)} %get-tuple-element.21, f32[1536]{0:T(1024)S(1)} %copy-done.5, f32[256]{0:T(256)S(1)} %add_rsqrt_fusion.1), kind=kOutput, calls=%fused_computation.37 | convolution fusion | flops 454557696 | bytes 3152896 | tf_op jit(solution)/shard_map/dot_general | solution.py:26
  86.6 3.9 %convolution_convert_fusion = bf16[256,1536]{1,0:T(8,128)(2,1)S(1)} fusion(bf16[576,1536]{1,0:T(8,128)(2,1)S(1)} %copy-done, bf16[1536,576]{0,1:T(8,128)(2,1)} %param.26, f32[256,576]{0,1:T(8,128)} %fusion.25, bf16[256,1536]{1,0:T(8,128)(2,1)S(1)} %get-tuple-element.21, f32[1536]{0:T(1024)S(1)} %copy-done.5, f32[256]{0:T(256)S(1)} %add_rsqrt_fusion.1), kind=kOutput, calls=%fused_computation.3 | convolution fusion | flops 909410304 | bytes 5708800 | tf_op jit(solution)/shard_map/dot_general | solution.py:29
  90.6 17.8 %shard_map.139 = f32[32,1536]{1,0:T(8,128)S(1)} custom-call(bf16[8,32,1536]{2,1,0:T(8,128)(2,1)S(1)} %bitcast.105), custom_call_target="tpu_custom_call" | custom-call | tf_op jit(solution)/shard_map/pallas_call | solution.py:344
  108.7 7.0 %all_to_all.10 = bf16[4,4,2,1536]{3,2,0,1:T(2,128)(2,1)S(1)} all-to-all(bf16[4,4,2,1536]{3,2,0,1:T(2,128)(2,1)S(1)} %copy.46), channel_id=1, replica_groups=mesh['req'=4,'kv'=8] {'req'}, dimensions={1} | all-to-all | bytes 196608 | tf_op jit(solution)/shard_map/all_to_all | solution.py:533
  115.8 0.9 fusion.4
  (73 shorter events, 2.1 us)
Async XLA Ops:
  0.0 86.6 %copy-start = (bf16[576,1536]{1,0:T(8,128)(2,1)S(1)}, bf16[576,1536]{1,0:T(8,128)(2,1)}, u32[]{:S(2)}) copy-start(bf16[576,1536]{1,0:T(8,128)(2,1)} %param.27) | copy-start | bytes 5308420
  2.3 8.4 %copy-start.1 = (s32[32]{0:T(128)S(1)}, s32[32]{0:T(128)}, u32[]{:S(2)}) copy-start(s32[32]{0:T(128)} %param.15) | copy-start | bytes 388
  3.0 8.5 %all-to-all-start = ((bf16[4,4,2,1536]{3,2,0,1:T(2,128)(2,1)}), bf16[4,4,2,1536]{3,2,0,1:T(2,128)(2,1)S(1)}, u32[]{:S(2)}, u32[]{:S(2)}) async-start(bf16[4,4,2,1536]{3,2,0,1:T(2,128)(2,1)} %copy.38), calls=%async_computation | async-start | bytes 196608 | tf_op jit(solution)/shard_map/all_to_all | solution.py:533
  11.3 20.4 %copy-start.3 = (f32[1536]{0:T(1024)S(1)}, f32[1536]{0:T(1024)}, u32[]{:S(2)}) copy-start(f32[1536]{0:T(1024)} %param.20) | copy-start | bytes 18436
  11.9 20.1 %copy-start.2 = (bf16[1536,256]{1,0:T(8,128)(2,1)S(1)}, bf16[1536,256]{1,0:T(8,128)(2,1)}, u32[]{:S(2)}) copy-start(bf16[1536,256]{1,0:T(8,128)(2,1)} %param.22) | copy-start | bytes 2359300
  32.4 51.1 %slice-start = ((s8[4718592]{0:T(1024)(128)(4,1)}), s8[4194304]{0:T(1024)(128)(4,1)S(1)}, s32[]{:S(2)}) async-start(s8[4718592]{0:T(1024)(128)(4,1)} %bitcast.117), calls=%async_computation.2 | async-start | bytes 8388608
  36.3 47.2 %slice-start.1 = ((s8[4718592]{0:T(1024)(128)(4,1)}), s8[524288]{0:T(1024)(128)(4,1)S(1)}, s32[]{:S(2)}) async-start(s8[4718592]{0:T(1024)(128)(4,1)} %bitcast.117), calls=%async_computation.3 | async-start | bytes 1048576
  83.5 1.5 %copy-start.4 = (bf16[1536,576]{0,1:T(8,128)(2,1)S(1)}, bf16[1536,576]{0,1:T(8,128)(2,1)}, u32[]{:S(2)}) copy-start(bf16[1536,576]{0,1:T(8,128)(2,1)} %param.25) | copy-start | bytes 5308420
  83.5 1.5 %copy-start.5 = (f32[1536]{0:T(1024)S(1)}, f32[1536]{0:T(1024)}, u32[]{:S(2)}) copy-start(f32[1536]{0:T(1024)} %param.24) | copy-start | bytes 18436
